TPU v7x, 32 devices: a whole 2x2x4 slice. The times are simulated.
32 devices in a mesh: dp: 16 (over z, y, core), mp: 2 (over x).
Axes of the slice: x: 2, y: 2, z: 4, core: 2. Of those that a mesh axis runs over, the one named last changes fastest.
Arguments:
- hidden_in: bfloat16 [16384, 1536], P(('dp', 'mp')), may hold values from -6 to 6
- positions: int32 [16384], P('dp'), may hold values from 0 to 511, as said below
- query_weight: bfloat16 [1536, 1536], P('dp', 'mp'), may hold values from -0.15625 to 0.15625
- query_bias: float32 [1536], replicated, may hold values from -3 to 3
- key_weight: bfloat16 [1536, 256], P('dp', 'mp'), may hold values from -0.15625 to 0.15625
- key_bias: float32 [256], replicated, may hold values from -3 to 3
- value_weight: bfloat16 [1536, 256], P('dp', 'mp'), may hold values from -0.15625 to 0.15625
- value_bias: float32 [256], replicated, may hold values from -3 to 3
- out_weight: bfloat16 [1536, 1536], P('mp', 'dp'), may hold values from -1.75 to 1.75
- gate_weight: bfloat16 [1536, 8960], P('dp', 'mp'), may hold values from -0.15625 to 0.15625
- up_weight: bfloat16 [1536, 8960], P('dp', 'mp'), may hold values from -0.15625 to 0.15625
- down_weight: bfloat16 [8960, 1536], P('mp', 'dp'), may hold values from -0.0625 to 0.0625
- attn_gain: float32 [1536], replicated, may hold values from 0.5 to 1.5
- ffn_gain: float32 [1536], replicated, may hold values from 0.5 to 1.5
- cotangent: bfloat16 [16384, 1536], P(('dp', 'mp')), may hold values from -6 to 6
Outputs:
- layer_out: bfloat16 [16384, 1536], P(('dp', 'mp'))
- grad_input: bfloat16 [16384, 1536], P(('dp', 'mp'))
- grad_query_weight: float32 [1536, 1536], P('dp', 'mp')
- grad_query_bias: float32 [1536], replicated
- grad_key_weight: float32 [1536, 256], P('dp', 'mp')
- grad_key_bias: float32 [256], replicated
- grad_value_weight: float32 [1536, 256], P('dp', 'mp')
- grad_value_bias: float32 [256], replicated
- grad_out_weight: float32 [1536, 1536], P('mp', 'dp')
- grad_gate_weight: float32 [1536, 8960], P('dp', 'mp')
- grad_up_weight: float32 [1536, 8960], P('dp', 'mp')
- grad_down_weight: float32 [8960, 1536], P('mp', 'dp')
- grad_attn_gain: float32 [1536], replicated
- grad_ffn_gain: float32 [1536], replicated
Inputs may be any that keep to these rules, and one draw needn't show every extreme that they name: `positions`: positions count up by one from 0 within each packed document; each sequence of 1024 tokens begins with a position 0, and its longest document has 512 tokens.
All inputs are finite; a program needn't handle non-finite values.
Results may differ from a plain program's by a relative error of at most 0.02.
Values may be sent and summed in bfloat16 or wider, within the bound.
A program may use at most 320 MiB of HBM per device.

v0:
```python
import math

import jax
import jax.numpy as jnp
from jax import lax
from jax.sharding import PartitionSpec as P

HD = 128
SEQ_LEN = 1024


EPS = 1e-06
ROPE_BASE = 1000000.0


def contract(left, right, left_dim, right_dim):
    return lax.dot_general(
        left, right, (((left_dim,), (right_dim,)), ((), ())), preferred_element_type=jnp.float32
    )


def normalize(values, gain):
    factor = lax.rsqrt(jnp.mean(values * values, axis=-1, keepdims=True) + EPS)
    return (values * factor * gain, factor)


def normalize_back(values, factor, gain, incoming):
    unit = values * factor
    scaled = incoming * gain
    gain_grad = jnp.sum(incoming * unit, axis=0)
    inner = jnp.mean(scaled * unit, axis=-1, keepdims=True)
    return (factor * (scaled - unit * inner), gain_grad)


def rotary(positions):
    half = HD // 2
    freq = jnp.power(ROPE_BASE, -2.0 * jnp.arange(half, dtype=jnp.float32) / HD)
    angles = positions.astype(jnp.float32)[:, None] * freq[None, :]
    return (jnp.cos(angles)[:, None, :], jnp.sin(angles)[:, None, :])


def rotate(values, cosines, sines):
    half = values.shape[-1] // 2
    first = values[..., :half]
    second = values[..., half:]
    return jnp.concatenate(
        [first * cosines - second * sines, second * cosines + first * sines], axis=-1
    )


def place_part(part, total, index):
    return lax.dynamic_update_slice_in_dim(
        jnp.zeros((total,), jnp.float32), part, index * part.shape[0], 0
    )


def body(
    hidden_in,
    positions,
    query_weight,
    query_bias,
    key_weight,
    key_bias,
    value_weight,
    value_bias,
    out_weight,
    gate_weight,
    up_weight,
    down_weight,
    attn_gain,
    ffn_gain,
    cotangent,
):
    group = positions.shape[0]
    seq_count = group // SEQ_LEN
    block = min(512, SEQ_LEN)
    block_count = SEQ_LEN // block
    heads = query_weight.shape[1] // HD
    width_q = heads * HD
    factor_q = 1.0 / math.sqrt(HD)
    shard = lax.axis_index("mp")
    bias_query = lax.dynamic_slice_in_dim(query_bias, shard * width_q, width_q, 0)
    bias_key = lax.dynamic_slice_in_dim(key_bias, shard * HD, HD, 0)
    bias_value = lax.dynamic_slice_in_dim(value_bias, shard * HD, HD, 0)
    query_full, key_full, value_full, out_full = (
        lax.all_gather(query_weight, "dp", axis=0, tiled=True),
        lax.all_gather(key_weight, "dp", axis=0, tiled=True),
        lax.all_gather(value_weight, "dp", axis=0, tiled=True),
        lax.all_gather(out_weight, "dp", axis=1, tiled=True),
    )
    residual = hidden_in.astype(jnp.float32)
    normed_one, factor_one = normalize(residual, attn_gain)
    inputs_one = lax.all_gather(normed_one.astype(jnp.bfloat16), "mp", axis=0, tiled=True)
    cosines, sines = rotary(positions)
    docs = jnp.cumsum(
        (positions == 0).astype(jnp.int32).reshape(seq_count, SEQ_LEN), axis=1
    ).reshape(group)
    queries_rot = rotate(
        (contract(inputs_one, query_full, 1, 0) + bias_query).reshape(group, heads, HD),
        cosines,
        sines,
    ).astype(jnp.bfloat16)
    keys_rot = rotate(
        (contract(inputs_one, key_full, 1, 0) + bias_key).reshape(group, 1, HD), cosines, sines
    )[:, 0].astype(jnp.bfloat16)
    values_low = (contract(inputs_one, value_full, 1, 0) + bias_value).astype(jnp.bfloat16)

    def visible_mask(start):
        doc_rows = lax.dynamic_slice_in_dim(docs, start, block, 0)
        rows = start + jnp.arange(block, dtype=jnp.int32)
        columns = jnp.arange(SEQ_LEN, dtype=jnp.int32)
        return (doc_rows[:, None] == docs[None, :]) & (columns[None, :] <= rows[:, None])

    def block_inputs(index):
        seq = index // block_count
        start = index % block_count * block
        base = seq * SEQ_LEN
        query_block = lax.dynamic_slice_in_dim(queries_rot, base + start, block, 0)
        return (seq, start, base, query_block, keys_rot, values_low)

    def attend_block(index):
        seq, start, base, query_block, key_seq, value_seq = block_inputs(index)
        scores = (
            jnp.einsum("qhd,kd->hqk", query_block, key_seq, preferred_element_type=jnp.float32)
            * factor_q
        )
        masked = jnp.where(visible_mask(start)[None], scores, -1e30)
        top = jnp.max(masked, axis=-1, keepdims=True)
        weights = jnp.exp(masked - top)
        total = jnp.sum(weights, axis=-1, keepdims=True)
        probs = (weights / total).astype(jnp.bfloat16)
        mixed = jnp.einsum("hqk,kd->qhd", probs, value_seq, preferred_element_type=jnp.float32)
        return (mixed.reshape(block, width_q), (top + jnp.log(total))[..., 0])

    block_ids = jnp.arange(seq_count * block_count, dtype=jnp.int32)
    mixed_all, log_totals = lax.map(attend_block, block_ids)
    mixed_low = mixed_all.reshape(group, width_q).astype(jnp.bfloat16)
    rows = mixed_low
    middle = residual + lax.psum_scatter(
        contract(rows, out_full, 1, 0), "mp", scatter_dimension=0, tiled=True
    )
    gate_full, up_full, down_full = (
        lax.all_gather(gate_weight, "dp", axis=0, tiled=True),
        lax.all_gather(up_weight, "dp", axis=0, tiled=True),
        lax.all_gather(down_weight, "dp", axis=1, tiled=True),
    )
    normed_two, factor_two = normalize(middle, ffn_gain)
    inputs_two = lax.all_gather(normed_two.astype(jnp.bfloat16), "mp", axis=0, tiled=True)
    gate = contract(inputs_two, gate_full, 1, 0)
    up = contract(inputs_two, up_full, 1, 0)
    sig = jax.nn.sigmoid(gate)
    swish = gate * sig
    hidden_low = (swish * up).astype(jnp.bfloat16)
    rows = hidden_low
    layer_out = (
        middle
        + lax.psum_scatter(
            contract(rows, down_full, 1, 0).astype(jnp.bfloat16),
            "mp",
            scatter_dimension=0,
            tiled=True,
        ).astype(jnp.float32)
    ).astype(jnp.bfloat16)
    query_back, key_back, value_back, out_back, gate_back, up_back, down_back = (
        lax.all_gather(query_weight, "dp", axis=0, tiled=True),
        lax.all_gather(key_weight, "dp", axis=0, tiled=True),
        lax.all_gather(value_weight, "dp", axis=0, tiled=True),
        lax.all_gather(out_weight, "dp", axis=1, tiled=True),
        lax.all_gather(gate_weight, "dp", axis=0, tiled=True),
        lax.all_gather(up_weight, "dp", axis=0, tiled=True),
        lax.all_gather(down_weight, "dp", axis=1, tiled=True),
    )
    grad_ffn = lax.all_gather(cotangent, "mp", axis=0, tiled=True)
    grad_hidden = contract(grad_ffn, down_back, 1, 1)
    grad_gate = (grad_hidden * up * sig * (1.0 + gate * (1.0 - sig))).astype(jnp.bfloat16)
    grad_up = (grad_hidden * swish).astype(jnp.bfloat16)
    sum_gate, sum_up, sum_down = (
        lax.psum_scatter(
            contract(inputs_two, grad_gate, 0, 0), "dp", scatter_dimension=0, tiled=True
        ),
        lax.psum_scatter(
            contract(inputs_two, grad_up, 0, 0), "dp", scatter_dimension=0, tiled=True
        ),
        lax.psum_scatter(
            contract(hidden_low, grad_ffn, 0, 0), "dp", scatter_dimension=1, tiled=True
        ),
    )
    grad_normed_two = lax.psum_scatter(
        contract(grad_gate, gate_back, 1, 1) + contract(grad_up, up_back, 1, 1),
        "mp",
        scatter_dimension=0,
        tiled=True,
    )
    through_two, gain_two = normalize_back(middle, factor_two, ffn_gain, grad_normed_two)
    grad_middle = cotangent.astype(jnp.float32) + through_two
    grad_attn = lax.all_gather(grad_middle.astype(jnp.bfloat16), "mp", axis=0, tiled=True)
    grad_out_local = contract(mixed_low, grad_attn, 0, 0)
    grad_mixed = contract(grad_attn, out_back, 1, 1).astype(jnp.bfloat16).reshape(group, heads, HD)

    def attend_back(index):
        seq, start, base, query_block, key_seq, value_seq = block_inputs(index)
        grad_block = lax.dynamic_slice_in_dim(grad_mixed, base + start, block, 0)
        scores = (
            jnp.einsum("qhd,kd->hqk", query_block, key_seq, preferred_element_type=jnp.float32)
            * factor_q
        )
        probs = jnp.where(
            visible_mask(start)[None], jnp.exp(scores - log_totals[index][..., None]), 0.0
        )
        grad_probs = jnp.einsum(
            "qhd,kd->hqk", grad_block, value_seq, preferred_element_type=jnp.float32
        )
        row_term = jnp.sum(probs * grad_probs, axis=-1, keepdims=True)
        grad_scores = (probs * (grad_probs - row_term)).astype(jnp.bfloat16)
        grad_query = (
            jnp.einsum("hqk,kd->qhd", grad_scores, key_seq, preferred_element_type=jnp.float32)
            * factor_q
        )
        grad_key = (
            jnp.einsum("hqk,qhd->kd", grad_scores, query_block, preferred_element_type=jnp.float32)
            * factor_q
        )
        grad_value = jnp.einsum(
            "hqk,qhd->kd",
            probs.astype(jnp.bfloat16),
            grad_block,
            preferred_element_type=jnp.float32,
        )
        return (grad_query, grad_key, grad_value)

    grad_query_blocks, grad_key_blocks, grad_value_blocks = lax.map(attend_back, block_ids)
    grad_keys_rot = jnp.sum(
        grad_key_blocks.reshape(seq_count, block_count, SEQ_LEN, HD), axis=1
    ).reshape(group, HD)
    grad_values = jnp.sum(
        grad_value_blocks.reshape(seq_count, block_count, SEQ_LEN, HD), axis=1
    ).reshape(group, HD)
    grad_queries = (
        rotate(grad_query_blocks.reshape(group, heads, HD), cosines, -sines)
        .reshape(group, width_q)
        .astype(jnp.bfloat16)
    )
    grad_keys = (
        rotate(grad_keys_rot.reshape(group, 1, HD), cosines, -sines)
        .reshape(group, HD)
        .astype(jnp.bfloat16)
    )
    grad_values_low = grad_values.astype(jnp.bfloat16)
    sum_query, sum_key, sum_value, sum_out = (
        lax.psum_scatter(
            contract(inputs_one, grad_queries, 0, 0), "dp", scatter_dimension=0, tiled=True
        ),
        lax.psum_scatter(
            contract(inputs_one, grad_keys, 0, 0), "dp", scatter_dimension=0, tiled=True
        ),
        lax.psum_scatter(
            contract(inputs_one, grad_values_low, 0, 0), "dp", scatter_dimension=0, tiled=True
        ),
        lax.psum_scatter(grad_out_local, "dp", scatter_dimension=1, tiled=True),
    )
    grad_normed_one = lax.psum_scatter(
        contract(grad_queries, query_back, 1, 1)
        + contract(grad_keys, key_back, 1, 1)
        + contract(grad_values_low, value_back, 1, 1),
        "mp",
        scatter_dimension=0,
        tiled=True,
    )
    through_one, gain_one = normalize_back(residual, factor_one, attn_gain, grad_normed_one)
    grad_input = (grad_middle + through_one).astype(jnp.bfloat16)
    bias_query_part = place_part(
        jnp.sum(grad_queries, axis=0, dtype=jnp.float32), query_bias.shape[0], shard
    )
    bias_key_part = place_part(
        jnp.sum(grad_keys, axis=0, dtype=jnp.float32), key_bias.shape[0], shard
    )
    bias_value_part = place_part(
        jnp.sum(grad_values_low, axis=0, dtype=jnp.float32), value_bias.shape[0], shard
    )
    gain_one_all, gain_two_all, query_bias_all, key_bias_all, value_bias_all = lax.psum(
        (gain_one, gain_two, bias_query_part, bias_key_part, bias_value_part), ("dp", "mp")
    )
    return (
        layer_out,
        grad_input,
        sum_query,
        query_bias_all,
        sum_key,
        key_bias_all,
        sum_value,
        value_bias_all,
        sum_out,
        sum_gate,
        sum_up,
        sum_down,
        gain_one_all,
        gain_two_all,
    )


def solution(mesh):
    return jax.shard_map(
        body,
        mesh=mesh,
        in_specs=(
            P(("dp", "mp"), None),
            P("dp"),
            P("dp", "mp"),
            P(),
            P("dp", "mp"),
            P(),
            P("dp", "mp"),
            P(),
            P("mp", "dp"),
            P("dp", "mp"),
            P("dp", "mp"),
            P("mp", "dp"),
            P(),
            P(),
            P(("dp", "mp"), None),
        ),
        out_specs=(
            P(("dp", "mp"), None),
            P(("dp", "mp"), None),
            P("dp", "mp"),
            P(),
            P("dp", "mp"),
            P(),
            P("dp", "mp"),
            P(),
            P("mp", "dp"),
            P("dp", "mp"),
            P("dp", "mp"),
            P("mp", "dp"),
            P(),
            P(),
        ),
        check_vma=False,
    )
```

profile of v0, /device:TPU:0, one launch (start us, length us, event | category | flops | bytes accessed | tf_op | source)
XLA Modules:
  0.0 2185.7 jit_solution(5147091181258785374)
XLA Ops:
  14.3 24.2 %all_gather.42 = bf16[1536,128]{1,0:T(8,128)(2,1)S(1)} all-gather(bf16[96,128]{1,0:T(8,128)(2,1)S(1)} %copy-done.47), channel_id=1, replica_groups=mesh['dp'=16,'mp'=2] {'dp'}, dimensions={0}, use_global_device_ids=true | all-gather | bytes 417792 | tf_op jit(solution)/shard_map/all_gather | solution.py:87
  69.3 35.7 %all-gather.12.cloned.1.call-done = bf16[1536,768]{1,0:T(8,128)(2,1)} async-done(((bf16[96,768]{1,0:T(8,128)(2,1)}), bf16[1536,768]{1,0:T(8,128)(2,1)}) %all-gather.12.cloned.1.call-update) | async-done | bytes 2359312 | tf_op jit(solution)/shard_map/all_gather | solution.py:86
  122.0 32.8 %while.30 = (s32[]{:T(128)}, bf16[2,512,768]{2,1,0:T(8,128)(2,1)}, f32[2,6,512]{2,1,0:T(8,128)S(1)}, s32[2]{0:T(128)S(1)}, s32[1024]{0:T(1024)S(1)}, /*index=5*/...) while((s32[]{:T(128)}, bf16[2,512,768]{2,1,0:T(8,128)(2,1)}, ...), condition=%wide.region_6.7_spmd, body=%wide.region_3.6_spmd.sunk | while | flops 1649931776 | bytes 46263272 | solution.py:136
  163.0 75.9 %reduce-scatter.12.cloned.1.call-done = f32[512,1536]{1,0:T(8,128)} async-done(((f32[1024,1536]{1,0:T(8,128)}), f32[512,1536]{1,0:T(8,128)}) %reduce-scatter.12.cloned.1.call-update) | async-done | bytes 3145744 | tf_op jit(solution)/shard_map/reduce_scatter | solution.py:139
  247.2 42.3 %all-gather.16.cloned.1.call-done = bf16[1024,1536]{1,0:T(8,128)(2,1)} async-done(((bf16[512,1536]{1,0:T(8,128)(2,1)}), bf16[1024,1536]{1,0:T(8,128)(2,1)}) %all-gather.16.cloned.1.call-update) | async-done | bytes 3145744 | tf_op jit(solution)/shard_map/all_gather | solution.py:148
  289.5 110.6 %all-gather.18.cloned.1.call-done = bf16[1536,4480]{1,0:T(8,128)(2,1)} async-done(((bf16[96,4480]{1,0:T(8,128)(2,1)}), bf16[1536,4480]{1,0:T(8,128)(2,1)}) %all-gather.18.cloned.1.call-update) | async-done | bytes 13762576 | tf_op jit(solution)/shard_map/all_gather | solution.py:143
  400.1 21.2 fusion.88
  421.3 87.7 %all-gather.20.cloned.1.call-done = bf16[1536,4480]{1,0:T(8,128)(2,1)} async-done(((bf16[96,4480]{1,0:T(8,128)(2,1)}), bf16[1536,4480]{1,0:T(8,128)(2,1)}) %all-gather.20.cloned.1.call-update) | async-done | bytes 13762576 | tf_op jit(solution)/shard_map/all_gather | solution.py:144
  529.1 24.7 %all-gather.24.cloned.1.call-done = bf16[1024,1536]{1,0:T(8,128)(2,1)} async-done(((bf16[512,1536]{1,0:T(8,128)(2,1)}), bf16[1024,1536]{1,0:T(8,128)(2,1)}) %all-gather.24.cloned.1.call-update) | async-done | bytes 3145744 | tf_op jit(solution)/shard_map/all_gather | solution.py:173
  553.8 110.8 %all-gather.22.cloned.1.call-done = bf16[4480,1536]{0,1:T(8,128)(2,1)} async-done(((bf16[4480,96]{0,1:T(8,128)(2,1)}), bf16[4480,1536]{0,1:T(8,128)(2,1)}) %all-gather.22.cloned.1.call-update) | async-done | bytes 13762576 | tf_op jit(solution)/shard_map/all_gather | solution.py:145
  664.6 34.0 %multiply_convert_fusion = (bf16[1024,4480]{1,0:T(8,128)(2,1)}, bf16[1024,4480]{1,0:T(8,128)(2,1)}, bf16[1024,4480]{1,0:T(8,128)(2,1)}) fusion(f32[1024,4480]{1,0:T(8,128)} %fusion.88, f32[1024,4480]{1,0:T(8,128)} %fusion.89, bf16[1024,1536]{1,0:T(8,128)(2,1)} %all-gather.24.cloned.1.call-done, bf16[4480,1536]{0,1:T(8,128)(2,1)} %all-gather.22.cloned.1.call-done), kind=kOutput, calls=%fused_computation.56 | convolution fusion | flops 14161674240 | bytes 81133568 | tf_op jit(solution)/shard_map/dot_general | solution.py:17
  698.6 21.8 fusion.90
  739.5 75.3 %reduce-scatter.16.cloned.1.call-done = f32[512,1536]{1,0:T(8,128)} async-done(((f32[1024,1536]{1,0:T(8,128)}), f32[512,1536]{1,0:T(8,128)}) %reduce-scatter.16.cloned.1.call-update) | async-done | bytes 3145744 | tf_op jit(solution)/shard_map/reduce_scatter | solution.py:188
  821.1 44.9 %all-gather.26.cloned.1.call-done = bf16[1024,1536]{1,0:T(8,128)(2,1)} async-done(((bf16[512,1536]{1,0:T(8,128)(2,1)}), bf16[1024,1536]{1,0:T(8,128)(2,1)}) %all-gather.26.cloned.1.call-update) | async-done | bytes 3145744 | tf_op jit(solution)/shard_map/all_gather | solution.py:196
  873.1 78.8 %while.31 = (s32[]{:T(128)}, f32[2,512,6,128]{3,1,0,2:T(8,128)}, f32[2,1024,128]{2,1,0:T(8,128)}, f32[2,1024,128]{2,1,0:T(8,128)}, s32[2]{0:T(128)}, /*index=5*/...) while((s32[]{:T(128)}, f32[2,512,6,128]{3,1,0,2:T(8,128)}, ...), condition=%wide.region_14.15_spmd, body=%wide.region_12.14_spmd.sunk | while | flops 4075812352 | bytes 196451664 | solution.py:231
  976.3 21.2 convolution_convert_fusion
  1091.7 40.3 %all-reduce = (f32[1536]{0:T(1024)}, f32[256]{0:T(256)}, f32[256]{0:T(256)}, f32[1536]{0:T(1024)}, f32[1536]{0:T(1024)}) all-reduce(f32[1536]{0:T(1024)S(1)} %bitcast_dynamic-update-slice_fusion.2, f32[256]{0:T(256)S(1)} %dynamic_update_slice.44, f32[256]{0:T(256)S(1)} %dynamic_update_slice.45, ...), channel_id=1, replica_groups=mesh['dp'=16,'mp'=2] {'dp','mp'}, use_global_device_ids=true, to_apply=%region_21.22 | all-reduce | flops 5120 | bytes 40960 | tf_op jit(solution)/shard_map/psum | solution.py:280
  1138.3 21.7 reduce-scatter.22.cloned.1.call-done
  1160.1 60.0 %reduce-scatter.24.cloned.1.call-done = f32[96,128]{1,0:T(8,128)} async-done(((f32[1536,128]{1,0:T(8,128)}), f32[96,128]{1,0:T(8,128)}) %reduce-scatter.24.cloned.1.call-update) | async-done | bytes 49168 | tf_op jit(solution)/shard_map/reduce_scatter | solution.py:256
  1220.0 78.9 %reduce-scatter.26.cloned.1.call-done = f32[768,96]{0,1:T(8,128)} async-done(((f32[768,1536]{0,1:T(8,128)}), f32[768,96]{0,1:T(8,128)}) %reduce-scatter.26.cloned.1.call-update) | async-done | bytes 294928 | tf_op jit(solution)/shard_map/reduce_scatter | solution.py:259
  1298.9 79.4 %reduce-scatter.20.cloned.1.call-done = f32[96,768]{1,0:T(8,128)} async-done(((f32[1536,768]{1,0:T(8,128)}), f32[96,768]{1,0:T(8,128)}) %reduce-scatter.20.cloned.1.call-update) | async-done | bytes 294928 | tf_op jit(solution)/shard_map/reduce_scatter | solution.py:250
  1378.3 266.4 %reduce-scatter.28.cloned.1.call-done = f32[96,4480]{1,0:T(8,128)} async-done(((f32[1536,4480]{1,0:T(8,128)}), f32[96,4480]{1,0:T(8,128)}) %reduce-scatter.28.cloned.1.call-update) | async-done | bytes 1720336 | tf_op jit(solution)/shard_map/reduce_scatter | solution.py:178
  1644.7 267.2 %reduce-scatter.30.cloned.1.call-done = f32[96,4480]{1,0:T(8,128)} async-done(((f32[1536,4480]{1,0:T(8,128)}), f32[96,4480]{1,0:T(8,128)}) %reduce-scatter.30.cloned.1.call-update) | async-done | bytes 1720336 | tf_op jit(solution)/shard_map/reduce_scatter | solution.py:181
  1911.9 266.5 %reduce-scatter.32.cloned.1.call-done = f32[4480,96]{0,1:T(8,128)} async-done(((f32[4480,1536]{0,1:T(8,128)}), f32[4480,96]{0,1:T(8,128)}) %reduce-scatter.32.cloned.1.call-update) | async-done | bytes 1720336 | tf_op jit(solution)/shard_map/reduce_scatter | solution.py:184
  (320 shorter events, 345.0 us)
Async XLA Ops:
  7.2 53.8 %all-gather.10.cloned.1.call-start = ((), (), s32[]{:S(2)}) async-start(), calls=%async_computation.11 | async-start | bytes 4718592 | tf_op jit(solution)/shard_map/all_gather | solution.py:93
  12.7 92.3 %all-gather.12.cloned.1.call-start = ((), (), s32[]{:S(2)}) async-start(), calls=%async_computation.12 | async-start | bytes 2506752 | tf_op jit(solution)/shard_map/all_gather | solution.py:86
  13.5 141.3 %all-gather.14.cloned.1.call-start = ((), (), s32[]{:S(2)}) async-start(), calls=%async_computation.13 | async-start | bytes 2506752 | tf_op jit(solution)/shard_map/all_gather | solution.py:89
  14.2 224.7 %reduce-scatter.12.cloned.1.call-start = ((), (), s32[]{:S(2)}) async-start(), calls=%async_computation.14 | async-start | bytes 9437184 | tf_op jit(solution)/shard_map/reduce_scatter | solution.py:139
  163.0 79.9 %copy-start.35 = (f32[1536]{0:T(1024)S(1)}, f32[1536]{0:T(1024)}, u32[]{:S(2)}) copy-start(f32[1536]{0:T(1024)} %param.32) | copy-start | bytes 18436
  163.0 126.5 %all-gather.16.cloned.1.call-start = ((), (), s32[]{:S(2)}) async-start(), calls=%async_computation.15 | async-start | bytes 4718592 | tf_op jit(solution)/shard_map/all_gather | solution.py:148
  244.4 155.7 %all-gather.18.cloned.1.call-start = ((), (), s32[]{:S(2)}) async-start(), calls=%async_computation.16 | async-start | bytes 14622720 | tf_op jit(solution)/shard_map/all_gather | solution.py:143
  245.0 264.1 %all-gather.20.cloned.1.call-start = ((), (), s32[]{:S(2)}) async-start(), calls=%async_computation.17 | async-start | bytes 14622720 | tf_op jit(solution)/shard_map/all_gather | solution.py:144
  245.7 308.1 %all-gather.24.cloned.1.call-start = ((), (), s32[]{:S(2)}) async-start(), calls=%async_computation.20 | async-start | bytes 4718592 | tf_op jit(solution)/shard_map/all_gather | solution.py:173
  246.5 418.1 %all-gather.22.cloned.1.call-start = ((), (), s32[]{:S(2)}) async-start(), calls=%async_computation.18 | async-start | bytes 14622720 | tf_op jit(solution)/shard_map/all_gather | solution.py:145
  247.2 567.7 %reduce-scatter.16.cloned.1.call-start = ((), (), s32[]{:S(2)}) async-start(), calls=%async_computation.21 | async-start | bytes 9437184 | tf_op jit(solution)/shard_map/reduce_scatter | solution.py:188
  289.5 219.5 %copy-start.56 = (bf16[1024,1536]{1,0:T(8,128)(2,1)S(1)}, bf16[1024,1536]{1,0:T(8,128)(2,1)}, u32[]{:S(2)}) copy-start(bf16[1024,1536]{1,0:T(8,128)(2,1)} %all-gather.16.cloned.1.call-done) | copy-start | bytes 9437188
  739.5 126.6 %all-gather.26.cloned.1.call-start = ((), (), s32[]{:S(2)}) async-start(), calls=%async_computation.22 | async-start | bytes 4718592 | tf_op jit(solution)/shard_map/all_gather | solution.py:196
  821.0 267.4 %reduce-scatter.18.cloned.1.call-start = ((), (), s32[]{:S(2)}) async-start(), calls=%async_computation.23 | async-start | bytes 9437184 | tf_op jit(solution)/shard_map/reduce_scatter | solution.py:261
  873.0 83.2 %copy-start.40 = (f32[1024]{0:T(1024)S(1)}, f32[1024]{0:T(1024)}, u32[]{:S(2)}) copy-start(f32[1024]{0:T(1024)} %copy-done.39) | copy-start | bytes 12292
  873.1 83.1 %copy-start.53 = (f32[64]{0:T(128)S(1)}, f32[64]{0:T(128)}, u32[]{:S(2)}) copy-start(f32[64]{0:T(128)} %copy-done.52) | copy-start | bytes 772
  976.2 155.8 %reduce-scatter.14.cloned.1.call-start = ((), (), s32[]{:S(2)}) async-start(), calls=%async_computation.19 | async-start | bytes 4718592 | tf_op jit(solution)/shard_map/reduce_scatter | solution.py:157
  997.5 162.5 %reduce-scatter.22.cloned.1.call-start = ((), (), s32[]{:S(2)}) async-start(), calls=%async_computation.25 | async-start | bytes 835584 | tf_op jit(solution)/shard_map/reduce_scatter | solution.py:253
  1002.3 217.7 %reduce-scatter.24.cloned.1.call-start = ((), (), s32[]{:S(2)}) async-start(), calls=%async_computation.26 | async-start | bytes 835584 | tf_op jit(solution)/shard_map/reduce_scatter | solution.py:256
  1004.5 294.4 %reduce-scatter.26.cloned.1.call-start = ((), (), s32[]{:S(2)}) async-start(), calls=%async_computation.27 | async-start | bytes 5013504 | tf_op jit(solution)/shard_map/reduce_scatter | solution.py:259
  1011.7 366.6 %reduce-scatter.20.cloned.1.call-start = ((), (), s32[]{:S(2)}) async-start(), calls=%async_computation.24 | async-start | bytes 5013504 | tf_op jit(solution)/shard_map/reduce_scatter | solution.py:250
  1017.6 627.2 %reduce-scatter.28.cloned.1.call-start = ((), (), s32[]{:S(2)}) async-start(), calls=%async_computation.28 | async-start | bytes 29245440 | tf_op jit(solution)/shard_map/reduce_scatter | solution.py:178
  1040.4 871.5 %reduce-scatter.30.cloned.1.call-start = ((), (), s32[]{:S(2)}) async-start(), calls=%async_computation.29 | async-start | bytes 29245440 | tf_op jit(solution)/shard_map/reduce_scatter | solution.py:181
  1061.4 1117.0 %reduce-scatter.32.cloned.1.call-start = ((), (), s32[]{:S(2)}) async-start(), calls=%async_computation.30 | async-start | bytes 29245440 | tf_op jit(solution)/shard_map/reduce_scatter | solution.py:184
  (74 other events, 1423.9 us)
Sparse Core Ops, SparseCore 0:
  12.8 47.6 all-gather.9
  62.8 42.2 all-gather.11
  107.3 41.0 all-gather.13
  163.1 75.7 reduce-scatter.11
  244.5 44.9 all-gather.15
  291.9 108.1 all-gather.17
  402.7 106.3 all-gather.19
  510.7 43.0 all-gather.23
  556.4 108.1 all-gather.21
  739.6 75.2 reduce-scatter.15
  821.1 44.9 all-gather.25
  976.3 77.0 reduce-scatter.17
  1055.8 43.3 reduce-scatter.13
  1103.1 56.8 reduce-scatter.21
  1164.4 55.5 reduce-scatter.23
  1224.3 74.5 reduce-scatter.25
  1303.7 74.5 reduce-scatter.19
  1382.8 261.8 reduce-scatter.27
  1650.0 261.8 reduce-scatter.29
  1916.5 261.9 reduce-scatter.31
where the time goes:
time: 2190 us
  waiting for transfers between devices  1650 us (75%)
  matrix products  321 us (15%)
  blocking collectives  83 us (4%)
  other arithmetic  63.1 us (3%)
  local copies, waits for them, and re-layouts  35.2 us (2%)
    reduce_scatter x1, waiting for transfers between devices, body(): lax.psum_scatter(contract(inputs_two, grad_up, 0, 0), 'dp', scatter_dimen...  267 us
    reduce_scatter x1, waiting for transfers between devices, body(): lax.psum_scatter(contract(hidden_low, grad_ffn, 0, 0), 'dp', scatter_dime...  266 us
    reduce_scatter x1, waiting for transfers between devices, body(): lax.psum_scatter(contract(inputs_two, grad_gate, 0, 0), 'dp', scatter_dim...  266 us
    dot_general x21, matrix products, contract(): lax.dot_general(left, right, (((left_dim,), (right_dim,)), ((), ())), pre...  256 us
    all_gather x1, waiting for transfers between devices, body(): lax.all_gather(down_weight, 'dp', axis=1, tiled=True)  111 us
    all_gather x1, waiting for transfers between devices, body(): lax.all_gather(gate_weight, 'dp', axis=0, tiled=True)  111 us
    all_gather x1, waiting for transfers between devices, body(): lax.all_gather(up_weight, 'dp', axis=0, tiled=True)  87.7 us
    reduce_scatter x1, waiting for transfers between devices, body(): lax.psum_scatter(contract(inputs_one, grad_queries, 0, 0), 'dp', scatter_...  79.4 us
  transfers between devices with their start and end apart: 20, of which 16 were waited for; matrix products, arithmetic and copies ran while one was open for 10% of the time, Pallas kernels for 0%

commit v1 on v0

v1 whole, which is shorter than its diff:
```python
import functools
import math

import jax
import jax.numpy as jnp
from jax import lax
from jax.experimental import pallas as pl
from jax.experimental.pallas import tpu as pltpu
from jax.sharding import PartitionSpec as P

HD = 128
SEQ_LEN = 1024
DOC_MAX = 512
EPS = 1e-06
ROPE_BASE = 1000000.0
BLOCK = 256
SCALE = 1.0 / math.sqrt(HD)
F32 = jnp.float32
BF16 = jnp.bfloat16


def contract(left, right, left_dim, right_dim):
    return lax.dot_general(
        left, right, (((left_dim,), (right_dim,)), ((), ())), preferred_element_type=F32
    )


def key_range(block_id):
    low = max(0, block_id * BLOCK - (DOC_MAX - 1)) // BLOCK * BLOCK
    return low, (block_id + 1) * BLOCK


def visible(start_row, low, high, block_id):
    keys = low + lax.broadcasted_iota(jnp.int32, (high - low, BLOCK), 0)
    queries = block_id * BLOCK + lax.broadcasted_iota(jnp.int32, (high - low, BLOCK), 1)
    return (keys >= start_row) & (keys <= queries)


def turn(values, cosines, sines):
    return values * cosines + pltpu.roll(values, HD // 2, 1) * sines


def attend_kernel(
    q_ref, k_ref, v_ref, bq_ref, bk_ref, bv_ref, cos_ref, sin_ref, start_ref,
    mixed_ref, qrot_ref, krot_ref, vlow_ref, lse_ref,
):
    head = pl.program_id(0)

    @pl.when(head == 0)
    def _():
        krot_ref[...] = turn(k_ref[...] + bk_ref[...], cos_ref[...], sin_ref[...]).astype(BF16)
        vlow_ref[...] = (v_ref[...] + bv_ref[...]).astype(BF16)

    qrot_ref[...] = turn(q_ref[...] + bq_ref[...], cos_ref[...], sin_ref[...]).astype(BF16)
    for i in range(SEQ_LEN // BLOCK):
        low, high = key_range(i)
        rows = pl.ds(i * BLOCK, BLOCK)
        start_row = start_ref[0:1, rows]
        scores = contract(krot_ref[low:high, :], qrot_ref[rows, :], 1, 1) * SCALE
        scores = jnp.where(visible(start_row, low, high, i), scores, -1e30)
        top = jnp.max(scores, axis=0, keepdims=True)
        weights = jnp.exp(scores - top)
        total = jnp.sum(weights, axis=0, keepdims=True)
        probs = (weights * (1.0 / total)).astype(BF16)
        mixed_ref[rows, :] = contract(probs, vlow_ref[low:high, :], 0, 0).astype(BF16)
        lse_ref[0, 0:1, rows] = top + jnp.log(total)


def attend(qkv, bias, cos2, sin2, start, heads):
    seq = SEQ_LEN
    full = lambda shape: pl.BlockSpec(shape, lambda h: (0,) * len(shape))
    col = lambda: pl.BlockSpec((seq, HD), lambda h: (0, h))
    at = lambda j: pl.BlockSpec((seq, HD), lambda h: (0, j))
    bat = lambda j: pl.BlockSpec((1, HD), lambda h: (0, j))
    return pl.pallas_call(
        attend_kernel,
        grid=(heads,),
        in_specs=[
            col(), at(heads), at(heads + 1),
            pl.BlockSpec((1, HD), lambda h: (0, h)), bat(heads), bat(heads + 1),
            full((seq, HD)), full((seq, HD)), full((1, seq)),
        ],
        out_specs=[
            col(), col(), full((seq, HD)), full((seq, HD)),
            pl.BlockSpec((1, 8, seq), lambda h: (h, 0, 0)),
        ],
        out_shape=[
            jax.ShapeDtypeStruct((seq, heads * HD), BF16),
            jax.ShapeDtypeStruct((seq, heads * HD), BF16),
            jax.ShapeDtypeStruct((seq, HD), BF16),
            jax.ShapeDtypeStruct((seq, HD), BF16),
            jax.ShapeDtypeStruct((heads, 8, seq), F32),
        ],
        compiler_params=pltpu.CompilerParams(vmem_limit_bytes=40 * 2**20),
        cost_estimate=pl.CostEstimate(
            flops=4 * heads * seq * seq * HD, bytes_accessed=10 * 2**20,
            transcendentals=heads * seq * seq // 2,
        ),
        name="attend",
    )(qkv, qkv, qkv, bias, bias, bias, cos2, sin2, start)


def attend_back_kernel(
    heads, qrot_ref, krot_ref, vlow_ref, lse_ref, grad_ref, cos_ref, sin_ref, start_ref,
    out_ref, gk_ref, gv_ref,
):
    head = pl.program_id(0)

    @pl.when(head == 0)
    def _():
        gk_ref[...] = jnp.zeros_like(gk_ref)
        gv_ref[...] = jnp.zeros_like(gv_ref)

    for i in range(SEQ_LEN // BLOCK):
        low, high = key_range(i)
        rows = pl.ds(i * BLOCK, BLOCK)
        start_row = start_ref[0:1, rows]
        query, grad = qrot_ref[rows, :], grad_ref[rows, :]
        keys = krot_ref[low:high, :]
        scores = contract(keys, query, 1, 1) * SCALE
        probs = jnp.where(
            visible(start_row, low, high, i), jnp.exp(scores - lse_ref[0, 0:1, rows]), 0.0
        )
        grad_probs = contract(vlow_ref[low:high, :], grad, 1, 1)
        row_term = jnp.sum(probs * grad_probs, axis=0, keepdims=True)
        grad_scores = (probs * (grad_probs - row_term)).astype(BF16)
        gk_ref[low:high, :] += contract(grad_scores, query, 1, 0)
        gv_ref[low:high, :] += contract(probs.astype(BF16), grad, 1, 0)
        grad_query = contract(grad_scores, keys, 0, 0) * SCALE
        out_ref[rows, pl.ds(pl.multiple_of(head * HD, HD), HD)] = turn(
            grad_query, cos_ref[rows, :], -sin_ref[rows, :]
        ).astype(BF16)

    @pl.when(head == heads - 1)
    def _():
        out_ref[:, heads * HD : (heads + 1) * HD] = turn(
            gk_ref[...] * SCALE, cos_ref[...], -sin_ref[...]
        ).astype(BF16)
        out_ref[:, (heads + 1) * HD :] = gv_ref[...].astype(BF16)


def attend_back(qrot, krot, vlow, lse, grad_mixed, cos2, sin2, start, heads):
    seq = SEQ_LEN
    full = lambda shape: pl.BlockSpec(shape, lambda h: (0,) * len(shape))
    col = lambda: pl.BlockSpec((seq, HD), lambda h: (0, h))
    return pl.pallas_call(
        functools.partial(attend_back_kernel, heads),
        grid=(heads,),
        in_specs=[
            col(), full((seq, HD)), full((seq, HD)),
            pl.BlockSpec((1, 8, seq), lambda h: (h, 0, 0)), col(),
            full((seq, HD)), full((seq, HD)), full((1, seq)),
        ],
        out_specs=full((seq, (heads + 2) * HD)),
        out_shape=jax.ShapeDtypeStruct((seq, (heads + 2) * HD), BF16),
        scratch_shapes=[pltpu.VMEM((seq, HD), F32), pltpu.VMEM((seq, HD), F32)],
        compiler_params=pltpu.CompilerParams(vmem_limit_bytes=40 * 2**20),
        cost_estimate=pl.CostEstimate(
            flops=10 * heads * seq * seq * HD, bytes_accessed=10 * 2**20,
            transcendentals=heads * seq * seq // 2,
        ),
        name="attend_back",
    )(qrot, krot, vlow, lse, grad_mixed, cos2, sin2, start)


class Ring:
    def __init__(self, members):
        self.members = members
        self.chips = members // 2
        self.half = self.chips // 2
        n = self.chips
        self.path = [2 * r if r < n // 2 else 2 * (n - 1 - r) + 1 for r in range(n)]
        self.offsets = [self.half]
        for k in range(self.half - 1, 0, -1):
            self.offsets += [k, n - k]
        self.offsets += [0]
        self.place = {k: i for i, k in enumerate(self.offsets)}

    def pairs(self, shift):
        n, path = self.chips, self.path
        return [
            (path[r] * 2 + c, path[(r + shift) % n] * 2 + c) for r in range(n) for c in range(2)
        ]

    def up(self, block):
        return lax.ppermute(block, "dp", self.pairs(1))

    def down(self, block):
        return lax.ppermute(block, "dp", self.pairs(-1))

    def across(self, block):
        return lax.ppermute(block, "dp", [(i, i ^ 1) for i in range(self.members)])

    def order(self):
        me = lax.axis_index("dp")
        path = jnp.array(self.path, jnp.int32)
        spot = jnp.zeros((self.chips,), jnp.int32).at[path].set(jnp.arange(self.chips, dtype=jnp.int32))
        mine = spot[me // 2]
        offsets = jnp.array(self.offsets, jnp.int32)
        chips = path[(mine + offsets) % self.chips]
        core = me % 2
        return jnp.concatenate([chips * 2 + core, chips * 2 + (1 - core)])

    def gather(self, block):
        n, h = self.chips, self.half
        rows = block.shape[0]
        got = {0: block}
        for k in range(1, h):
            got[n - k] = self.up(got[(n - k + 1) % n])
            got[k] = self.down(got[k - 1])
        first = self.up(got[h + 1][: rows // 2])
        second = self.down(got[h - 1][rows // 2 :])
        other = {k: self.across(got[k]) for k in got}
        got_half = [first, second]
        other_half = [self.across(first), self.across(second)]
        blocks = []
        for side, halves in ((got, got_half), (other, other_half)):
            for k in self.offsets:
                blocks.append(tuple(halves) if k == h else (side[k],))
        return blocks, first

    def reduce(self, own, rows):
        def term(k):
            begin = self.place[k] * rows
            return jnp.concatenate([o[begin : begin + rows] for o in own], axis=1)

        return self.reduce_terms(term, rows)

    def reduce_terms(self, term, rows):
        n, h = self.chips, self.half
        up = self.up(term(h)[: rows // 2])
        down = self.down(term(h)[rows // 2 :])
        for k in range(h - 1, 0, -1):
            mine_up, mine_down = term(k), term(n - k)
            if k == h - 1:
                sent_up = jnp.concatenate([
                    (up.astype(F32) + mine_up[: rows // 2].astype(F32)).astype(BF16),
                    mine_up[rows // 2 :],
                ])
                sent_down = jnp.concatenate([
                    mine_down[: rows // 2],
                    (down.astype(F32) + mine_down[rows // 2 :].astype(F32)).astype(BF16),
                ])
            else:
                sent_up = (up.astype(F32) + mine_up.astype(F32)).astype(BF16)
                sent_down = (down.astype(F32) + mine_down.astype(F32)).astype(BF16)
            up, down = self.up(sent_up), self.down(sent_down)
        return term(0).astype(F32) + up.astype(F32) + down.astype(F32)


def stack(blocks, begin, stop):
    return jnp.concatenate([part[:, begin:stop] for block in blocks for part in block], axis=0)


def swap(block):
    return lax.ppermute(block, "mp", [(0, 1), (1, 0)])


def rms(values):
    return lax.rsqrt(jnp.mean(values * values, axis=-1, keepdims=True) + EPS)


def after(value, *earlier):
    return lax.optimization_barrier((value, *earlier))[0]


def split_hidden(width, parts):
    tiles = width // HD
    cuts = [round(tiles * i / parts) * HD for i in range(parts + 1)]
    return list(zip(cuts[:-1], cuts[1:]))


def body_general(
    hidden_in, positions, query_weight, query_bias, key_weight, key_bias, value_weight, value_bias,
    out_weight, gate_weight, up_weight, down_weight, attn_gain, ffn_gain, cotangent,
):
    ring = Ring(lax.axis_size("dp"))
    rows = query_weight.shape[0]
    width = rows * ring.members
    side_rows = rows * ring.chips
    heads = query_weight.shape[1] // HD
    width_q = heads * HD
    width_qkv = width_q + 2 * HD
    own_tokens = hidden_in.shape[0]
    shard = lax.axis_index("mp")

    def whole(own, other):
        first = jnp.where(shard == 0, own, other)
        second = jnp.where(shard == 0, other, own)
        return jnp.concatenate([first, second], axis=0)

    def own_half(values):
        return lax.dynamic_slice_in_dim(values, shard * own_tokens, own_tokens, 0)

    def other_half(values):
        return lax.dynamic_slice_in_dim(values, (1 - shard) * own_tokens, own_tokens, 0)

    hidden_other = swap(hidden_in)
    attn_pack = jnp.concatenate([query_weight, key_weight, value_weight, out_weight.T], axis=1)
    attn_blocks, attn_last = ring.gather(attn_pack)
    cotangent_other = swap(after(cotangent, hidden_other))
    down_t = down_weight.T
    spans = split_hidden(gate_weight.shape[1], 2)
    ffn_blocks = []
    last = attn_last
    for begin, stop in spans:
        pack = jnp.concatenate(
            [gate_weight[:, begin:stop], up_weight[:, begin:stop], down_t[:, begin:stop]], axis=1
        )
        blocks, last = ring.gather(after(pack, last))
        ffn_blocks.append(blocks)

    order = ring.order()
    feature = (order[:, None] * rows + jnp.arange(rows, dtype=jnp.int32)[None, :]).reshape(width)
    shuffle = (jnp.arange(width, dtype=jnp.int32)[:, None] == feature[None, :]).astype(BF16)

    def to_order(values):
        return contract(values, shuffle, 1, 0).astype(BF16)

    def from_order(values):
        return contract(values, shuffle, 1, 1).astype(BF16)

    def vector_to_order(values):
        return jnp.sum(jnp.where(shuffle > 0, values[:, None], 0.0), axis=0)

    def vector_from_order(values):
        return jnp.sum(jnp.where(shuffle > 0, values[None, :], 0.0), axis=1)

    gain_attn, gain_ffn = vector_to_order(attn_gain), vector_to_order(ffn_gain)

    hidden_all = to_order(whole(hidden_in, hidden_other))
    resid_all = hidden_all.astype(F32)
    factor_one = rms(resid_all)
    inputs_one = (resid_all * factor_one * gain_attn).astype(BF16)
    half = HD // 2
    freq = jnp.power(ROPE_BASE, -2.0 * jnp.arange(half, dtype=F32) / HD)
    angles = positions.astype(F32)[:, None] * freq[None, :]
    cosines, sines = jnp.cos(angles), jnp.sin(angles)
    cos2 = jnp.concatenate([cosines, cosines], axis=1)
    sin2 = jnp.concatenate([-sines, sines], axis=1)
    start = (jnp.arange(SEQ_LEN, dtype=jnp.int32) - positions)[None, :]
    bias = jnp.concatenate([
        lax.dynamic_slice_in_dim(query_bias, shard * width_q, width_q, 0),
        lax.dynamic_slice_in_dim(key_bias, shard * HD, HD, 0),
        lax.dynamic_slice_in_dim(value_bias, shard * HD, HD, 0),
    ])[None, :]
    qkv_full = stack(attn_blocks, 0, width_qkv)
    out_full = stack(attn_blocks, width_qkv, width_qkv + width_q)
    qkv = contract(inputs_one, qkv_full, 1, 0)
    mixed, qrot, krot, vlow, lse = attend(qkv, bias, cos2, sin2, start, heads)
    out_other = swap(contract(other_half(mixed), out_full, 1, 1).astype(BF16))
    middle = (
        own_half(hidden_all).astype(F32)
        + contract(own_half(mixed), out_full, 1, 1)
        + out_other.astype(F32)
    )
    factor_two = rms(middle)
    in_two_own = (middle * factor_two * gain_ffn).astype(BF16)
    inputs_two = whole(in_two_own, swap(in_two_own))
    grad_ffn = to_order(whole(cotangent, cotangent_other))

    hiddens, grads_gate, grads_up, weights = [], [], [], []
    for (begin, stop), blocks in zip(spans, ffn_blocks):
        wide = stop - begin
        gate_full = stack(blocks, 0, wide)
        up_full = stack(blocks, wide, 2 * wide)
        down_full = stack(blocks, 2 * wide, 3 * wide)
        grad_hidden = contract(grad_ffn, down_full, 1, 0)
        gate = contract(inputs_two, gate_full, 1, 0)
        up = contract(inputs_two, up_full, 1, 0)
        sig = jax.nn.sigmoid(gate)
        swish = gate * sig
        hiddens.append((swish * up).astype(BF16))
        grads_gate.append((grad_hidden * up * sig * (1.0 + gate * (1.0 - sig))).astype(BF16))
        grads_up.append((grad_hidden * swish).astype(BF16))
        weights.append((gate_full, up_full, down_full))

    def side(values, index):
        return values[:, index * side_rows : (index + 1) * side_rows]

    def chip_sum(left, right):
        sent = contract(side(left, 1), right, 0, 0).astype(BF16)
        return (contract(side(left, 0), right, 0, 0) + ring.across(sent).astype(F32)).astype(BF16)

    sums = []
    for index in range(len(spans)):
        own = [
            chip_sum(inputs_two, grads_gate[index]),
            chip_sum(inputs_two, grads_up[index]),
            chip_sum(grad_ffn, hiddens[index]),
        ]
        sums.append(ring.reduce(own, rows))

    def back_two(take):
        total = None
        for (gate_full, up_full, _), g, u in zip(weights, grads_gate, grads_up):
            term = contract(take(g), gate_full, 1, 1) + contract(take(u), up_full, 1, 1)
            total = term if total is None else total + term
        return total

    def forward_out(take):
        total = None
        for (_, _, down_full), h in zip(weights, hiddens):
            term = contract(take(h), down_full, 1, 1)
            total = term if total is None else total + term
        return total

    back_other = swap(back_two(other_half).astype(BF16))
    grad_normed_two = back_two(own_half) + back_other.astype(F32)
    ffn_other = swap(forward_out(other_half).astype(BF16))
    layer_out = from_order(
        (middle + forward_out(own_half) + ffn_other.astype(F32)).astype(BF16)
    )

    unit_two = middle * factor_two
    scaled = grad_normed_two * gain_ffn
    gain_two = jnp.sum(grad_normed_two * unit_two, axis=0)
    inner = jnp.mean(scaled * unit_two, axis=-1, keepdims=True)
    grad_middle = own_half(grad_ffn).astype(F32) + factor_two * (scaled - unit_two * inner)

    grad_attn_own = grad_middle.astype(BF16)
    grad_attn = whole(grad_attn_own, swap(grad_attn_own))
    grad_mixed = contract(grad_attn, out_full, 1, 0).astype(BF16)
    grad_qkv = attend_back(qrot, krot, vlow, lse, grad_mixed, cos2, sin2, start, heads)
    sum_out = ring.reduce([chip_sum(grad_attn, mixed)], rows)
    sum_qkv = ring.reduce([chip_sum(inputs_one, grad_qkv)], rows)

    back_one_other = contract(other_half(grad_qkv), qkv_full, 1, 1)
    one_other = swap(back_one_other.astype(BF16))
    back_one_own = contract(own_half(grad_qkv), qkv_full, 1, 1)
    unit_all = resid_all * factor_one
    unit_one = own_half(unit_all)
    gain_one = jnp.sum(back_one_own * unit_one, axis=0) + jnp.sum(
        back_one_other * other_half(unit_all), axis=0
    )
    grad_normed_one = back_one_own + one_other.astype(F32)
    scaled_one = grad_normed_one * gain_attn
    inner_one = jnp.mean(scaled_one * unit_one, axis=-1, keepdims=True)
    through_one = own_half(factor_one) * (scaled_one - unit_one * inner_one)
    grad_input = from_order((grad_middle + through_one).astype(BF16))

    bias_part = jnp.sum(grad_qkv.astype(F32), axis=0)

    def place(part, total):
        return lax.dynamic_update_slice_in_dim(
            jnp.zeros((total,), F32), part, shard * part.shape[0], 0
        )

    small = jnp.concatenate([
        vector_from_order(gain_one),
        vector_from_order(gain_two),
        place(bias_part[:width_q], query_bias.shape[0]),
        place(bias_part[width_q : width_q + HD], key_bias.shape[0]),
        place(bias_part[width_q + HD :], value_bias.shape[0]),
    ])
    small = small + swap(small)
    bit = 1
    while bit < ring.members:
        small = small + lax.ppermute(small, "dp", [(i, i ^ bit) for i in range(ring.members)])
        bit *= 2
    cuts = [width, width, query_bias.shape[0], key_bias.shape[0], value_bias.shape[0]]
    pieces, begin = [], 0
    for cut in cuts:
        pieces.append(small[begin : begin + cut])
        begin += cut

    def gather_cols(index):
        parts = []
        for (begin, stop), total in zip(spans, sums):
            wide = stop - begin
            parts.append(total[:, index * wide : (index + 1) * wide])
        return jnp.concatenate(parts, axis=1)

    return (
        layer_out,
        grad_input,
        sum_qkv[:, :width_q],
        pieces[2],
        sum_qkv[:, width_q : width_q + HD],
        pieces[3],
        sum_qkv[:, width_q + HD :],
        pieces[4],
        sum_out.T,
        gather_cols(0),
        gather_cols(1),
        gather_cols(2).T,
        pieces[0],
        pieces[1],
    )


CHIPS = 8
HALF = CHIPS // 2
CHUNK = 512
TILE = 256
MESH = pl.DeviceIdType.MESH


class Spot:
    def __init__(self, rows):
        self.rows = rows
        self.me = lax.axis_index("dp")
        self.shard = lax.axis_index("mp")
        self.core = lax.rem(self.me, 2)
        chip = lax.div(self.me, 2)
        line, back = lax.div(chip, 2), lax.rem(chip, 2)
        self.spot = line * (1 - back) + (CHIPS - 1 - line) * back
        self.sibling = self.me + 1 - 2 * self.core
        self.next = (self.chip(1) * 2 + self.core, self.chip(CHIPS - 1) * 2 + self.core)

    def chip(self, offset):
        place = lax.rem(self.spot + offset, CHIPS)
        back = lax.div(place, HALF)
        return (1 - back) * (2 * place) + back * (2 * (CHIPS - 1 - place) + 1)

    def greet(self):
        barrier = pltpu.get_barrier_semaphore()
        for target in (
            {"dp": self.sibling}, {"dp": self.next[0]}, {"dp": self.next[1]}, {"mp": 1 - self.shard}
        ):
            pl.semaphore_signal(barrier, inc=1, device_id=target, device_id_type=MESH)
        pl.semaphore_wait(barrier, 4)

    def part(self, block, half=None):
        begin, size = block * self.rows, self.rows
        if half is not None:
            size = self.rows // 2
            begin = begin + half * size
        return pl.ds(pl.multiple_of(begin, 16), size)


def tile_of(index, size=TILE):
    return pl.ds(pl.multiple_of(index * size, size), size)


def small_inputs(ref, width_qkv, width):
    gains = width_qkv + width, width_qkv + 2 * width

    def start_of(block):
        begin = gains[1] + block * BLOCK
        return ref[0:1, begin : begin + BLOCK]

    return (
        ref[0:1, 0:width_qkv], ref[0:1, width_qkv : gains[0]], ref[0:1, gains[0] : gains[1]], start_of
    )


def visible_keys(start_row, low, high, block_id):
    shape = (high - low, BLOCK)
    keys = low + lax.broadcasted_iota(jnp.int32, shape, 0)
    queries = block_id * BLOCK + lax.broadcasted_iota(jnp.int32, shape, 1)
    return (keys.astype(F32) >= start_row) & (keys <= queries)


class Gather:
    def __init__(self, here, held, home, landed, hop_send, hop_recv, side_send, side_recv, store_sem):
        self.here, self.held, self.home, self.landed = here, held, home, landed
        self.hop_send, self.hop_recv = hop_send, hop_recv
        self.side_send, self.side_recv, self.store_sem = side_send, side_recv, store_sem

    def member(self, step, way, sibling=False):
        here = self.here
        chip = here.chip((CHIPS - step) % CHIPS if way == 0 else step)
        return chip * 2 + (1 - here.core if sibling else here.core)

    def hop(self, unit, step, way, arrival=False):
        half = way if step == HALF else None
        source = self.held(unit, step if arrival else step - 1, way, half)
        target = source if arrival or self.landed(unit) else self.held(unit, step, way, half)
        return pltpu.make_async_remote_copy(
            src_ref=source, dst_ref=target, send_sem=self.hop_send.at[unit, step - 1, way],
            recv_sem=self.hop_recv.at[unit, step - 1, way],
            device_id={"dp": self.here.next[way]}, device_id_type=MESH,
        )

    def index(self, step, way):
        return 0 if step == 0 else 2 * step - 1 + way

    def across(self, unit, step, way, arrival=False):
        half = way if step == HALF else None
        target = self.home(unit, self.member(step, way, sibling=arrival), half)
        source = target if arrival else self.held(unit, step, way, half)
        index = self.index(step, way)
        return pltpu.make_async_remote_copy(
            src_ref=source, dst_ref=target, send_sem=self.side_send.at[unit, index],
            recv_sem=self.side_recv.at[unit, index],
            device_id={"dp": self.here.sibling}, device_id_type=MESH,
        )

    def store(self, unit, step, way):
        half = way if step == HALF else None
        return pltpu.make_async_copy(
            self.held(unit, step, way, half), self.home(unit, self.member(step, way), half),
            self.store_sem.at[unit, self.index(step, way)],
        )

    def start(self, unit):
        for way in range(2):
            self.hop(unit, 1, way).start()
        self.across(unit, 0, 0).start()
        if not self.landed(unit):
            self.store(unit, 0, 0).start()

    def step(self, unit, step):
        for way in range(2):
            self.hop(unit, step - 1, way, arrival=True).wait_recv()
            if step <= HALF:
                self.hop(unit, step, way).start()
            self.across(unit, step - 1, way).start()
            if not self.landed(unit):
                self.store(unit, step - 1, way).start()

    def pieces(self):
        return [(0, 0)] + [(step, way) for step in range(1, HALF + 1) for way in range(2)]

    def end(self, unit):
        for step, way in self.pieces():
            self.across(unit, step, way, arrival=True).wait_recv()

    def sent(self, unit):
        for step, way in self.pieces():
            self.across(unit, step, way).wait_send()
            if step:
                self.hop(unit, step, way).wait_send()
            if not self.landed(unit):
                self.store(unit, step, way).wait()


def units_of(chunk, total):
    return min(CHUNK, total - chunk * CHUNK)


def pack_copies(weights, pack, chunks, sem):
    copies = []
    for i, chunk in enumerate(chunks):
        begin, size = chunk * CHUNK, units_of(chunk, weights[0].shape[1])
        for m, ref in enumerate(weights):
            copies.append(pltpu.make_async_copy(
                ref.at[:, begin : begin + size], pack.at[i, :, m * size : (m + 1) * size],
                sem.at[i, m],
            ))
    return copies


LATER = 3
PAIRS = 2
QUARTERS = 4


def forward_kernel(
    cfg, hid, cot, turns, places, bias_q, bias_k, bias_v, gain_a, gain_f,
    wq, wk, wv, wo, wg, wu, wd,
    w_ffn, w_attn, hid_all, cot_all, in_one_t, qrot, krot, vlow, mixed, lse, middle, in_two, vec_ref,
    cos_ref, sin_ref, in_two_t, cot_t,
    wa, qkv, psend, precv, pack, slots, in_one, cots, turned, turned_cot,
    local_sem, pack_sem, store_sem, hop_send, hop_recv, side_send, side_recv, x_send, x_recv, t_sem,
):
    rows, heads, units = cfg
    own_tokens, width = hid.shape
    tokens = 2 * own_tokens
    width_q = heads * HD
    width_qkv = width_q + 2 * HD
    here = Spot(rows)
    shard = here.shard

    own_rows = pl.ds(pl.multiple_of(shard * own_tokens, TILE), own_tokens)
    other_rows = pl.ds(pl.multiple_of((1 - shard) * own_tokens, TILE), own_tokens)
    quarter = own_tokens // QUARTERS

    def quarter_rows(index, side):
        return pl.ds(pl.multiple_of(side * own_tokens + index * quarter, quarter), quarter)

    mine = here.part(here.me)
    attn_copies, column = [], 0
    for i, ref in enumerate((wq, wk, wv, wo)):
        wide = ref.shape[1]
        attn_copies.append(
            pltpu.make_async_copy(ref, wa.at[mine, column : column + wide], local_sem.at[i])
        )
        column += wide
    ffn_copies = pack_copies((wg, wu, wd), pack, range(PAIRS * units), pack_sem)
    own_copies = [
        pltpu.make_async_copy(hid, hid_all.at[own_rows, :], local_sem.at[4]),
        pltpu.make_async_copy(cot, cots.at[own_rows, :], local_sem.at[5]),
    ]
    for copy in attn_copies + own_copies + ffn_copies:
        copy.start()

    column = 0
    for ref in (bias_q, bias_k, bias_v):
        size = ref.shape[0] // 2
        row = ref[...].reshape(1, 2 * size)
        vec_ref[:, column : column + size] = jnp.where(shard == 0, row[:, :size], row[:, size:])
        column += size
    for ref in (gain_a, gain_f):
        vec_ref[:, column : column + width] = ref[...].reshape(1, width)
        column += width
    vec_ref[:, column : column + tokens] = (
        lax.broadcasted_iota(jnp.int32, (1, tokens), 1) - places[...].reshape(1, tokens)
    ).astype(F32)
    bias, gain_one, gain_two, start_of = small_inputs(vec_ref, width_qkv, width)

    here.greet()

    def swap_copy(index, src, dst):
        return pltpu.make_async_remote_copy(
            src_ref=src, dst_ref=dst, send_sem=x_send.at[index], recv_sem=x_recv.at[index],
            device_id={"mp": 1 - shard}, device_id_type=MESH,
        )

    hid_swap = (swap_copy(0, hid, hid_all.at[own_rows, :]), swap_copy(0, hid, hid_all.at[other_rows, :]))
    mix_swap = swap_copy(1, psend, precv)
    two_swap = (
        swap_copy(2, in_two.at[own_rows, :], in_two.at[own_rows, :]),
        swap_copy(2, in_two.at[other_rows, :], in_two.at[other_rows, :]),
    )

    def cot_swap(index, arrival=False):
        ref = cots.at[quarter_rows(index, 1 - shard if arrival else shard), :]
        return swap_copy(3 + index, ref, ref)

    def home(unit, member, half):
        part = here.part(member, half)
        if unit == 0:
            return wa.at[part, :]
        return w_ffn.at[(unit - 1) * PAIRS : unit * PAIRS, part, :]

    def held(unit, step, way, half):
        if unit == 0:
            return home(0, gather.member(step, way), half)
        part = slice(0, rows) if half is None else slice(half * rows // 2, (half + 1) * rows // 2)
        if step == 0:
            return pack.at[(unit - 1) * PAIRS : unit * PAIRS, part, :]
        slot = 2 * HALF - 2 if step == HALF else 2 * (step - 1) + way
        return slots.at[unit - 1, slot, :, part, :]

    gather = Gather(
        here, held, home, lambda unit: unit == 0, hop_send, hop_recv, side_send, side_recv, store_sem
    )
    ffn_units = range(1, units + 1)

    hid_swap[0].start()
    for copy in attn_copies:
        copy.wait()
    gather.start(0)
    at = jnp.broadcast_to(places[...].reshape(1, tokens).astype(F32), (HD, tokens)).T
    angles = at * turns[...].reshape(1, HD)
    cos_ref[...] = jnp.cos(angles)
    lanes = lax.broadcasted_iota(jnp.int32, (tokens, HD), 1)
    sin_ref[...] = jnp.where(lanes < HD // 2, -1.0, 1.0) * jnp.sin(angles)

    for step in range(2, HALF + 1):
        gather.step(0, step)
    for copy in ffn_copies:
        copy.wait()
    for unit in ffn_units:
        gather.start(unit)
    gather.step(0, HALF + 1)

    for copy in own_copies:
        copy.wait()
    hid_swap[1].wait_recv()
    for index in range(QUARTERS - 1):
        cot_swap(index).start()

    @pl.loop(0, tokens // TILE)
    def _(t):
        v = hid_all[tile_of(t), :].astype(F32)
        factor = lax.rsqrt(jnp.mean(v * v, axis=-1, keepdims=True) + EPS)
        in_one[tile_of(t), :] = (v * factor * gain_one).astype(BF16)

    gather.end(0)
    wa_out = pltpu.make_async_copy(wa, w_attn, local_sem.at[6])
    wa_out.start()

    @pl.loop(0, tokens // TILE)
    def _(t):
        part = tile_of(t)
        qkv[part, :] = contract(in_one[part, :], wa[:, 0:width_qkv], 1, 0) + bias
        cosines, sines = cos_ref[part, :], sin_ref[part, :]
        for h in range(heads):
            columns = slice(h * HD, (h + 1) * HD)
            qrot[part, columns] = turn(qkv[part, columns], cosines, sines).astype(BF16)
        krot[part, :] = turn(qkv[part, width_q : width_q + HD], cosines, sines).astype(BF16)
        vlow[part, :] = qkv[part, width_q + HD :].astype(BF16)

    def attend(blocks):
        @pl.loop(0, heads)
        def _(h):
            columns = tile_of(h, HD)
            for i in blocks:
                low, high = key_range(i)
                part = pl.ds(i * BLOCK, BLOCK)
                scores = contract(krot[low:high, :], qrot[part, columns], 1, 1) * SCALE
                scores = jnp.where(visible_keys(start_of(i), low, high, i), scores, -1e30)
                top = jnp.max(scores, axis=0, keepdims=True)
                weights = jnp.exp(scores - top)
                total = jnp.sum(weights, axis=0, keepdims=True)
                probs = (weights * (1.0 / total)).astype(BF16)
                mixed[part, columns] = contract(probs, vlow[low:high, :], 0, 0).astype(BF16)
                lse[h, 0:1, part] = top + jnp.log(total)

    halves = (range(own_tokens // BLOCK), range(own_tokens // BLOCK, tokens // BLOCK))
    for index in range(2):
        @pl.when(shard == index)
        def _():
            attend(halves[1 - index])

    @pl.loop(0, width // TILE)
    def _(n):
        weight = wa[tile_of(n), width_qkv:]
        psend[:, tile_of(n)] = contract(mixed[other_rows, :], weight, 1, 1).astype(BF16)

    mix_swap.start()
    for index in range(2):
        @pl.when(shard == index)
        def _():
            attend(halves[index])

    @pl.loop(0, width // TILE)
    def _(n):
        weight = wa[tile_of(n), width_qkv:]
        middle[:, tile_of(n)] = (
            contract(mixed[own_rows, :], weight, 1, 1) + hid[:, tile_of(n)].astype(F32)
        )

    for unit in ffn_units:
        gather.step(unit, 2)

    def transpose(source, target, first, begin, count):
        @pl.loop(0, width // TILE)
        def _(n):
            for t in range(count):
                part = pl.ds(pl.multiple_of(begin + t * TILE, TILE), TILE)
                target[tile_of(n), part] = source[part, tile_of(n)].T

    transpose(in_one, turned, 0, 0, tokens // TILE)
    one_turned = pltpu.make_async_copy(turned, in_one_t, t_sem.at[0])
    one_turned.start()
    mine_begin, theirs_begin = shard * own_tokens, (1 - shard) * own_tokens
    transpose(cots, turned_cot, 0, mine_begin, own_tokens // TILE)
    for index in range(QUARTERS // 2):
        cot_swap(index, arrival=True).wait_recv()
    transpose(cots, turned_cot, 0, theirs_begin, own_tokens // TILE // 2)

    mix_swap.wait_recv()

    @pl.loop(0, own_tokens // TILE)
    def _(t):
        part = tile_of(t)
        v = middle[part, :] + precv[part, :].astype(F32)
        middle[part, :] = v
        factor = lax.rsqrt(jnp.mean(v * v, axis=-1, keepdims=True) + EPS)
        to = pl.ds(pl.multiple_of(shard * own_tokens + t * TILE, TILE), TILE)
        in_two[to, :] = (v * factor * gain_two).astype(BF16)

    two_swap[0].start()
    cot_swap(QUARTERS - 1).start()
    one_turned.wait()
    for unit in ffn_units:
        gather.step(unit, 3)
    transpose(in_two, turned, 0, mine_begin, own_tokens // TILE)
    for unit in list(ffn_units)[:1]:
        gather.step(unit, 4)
    two_swap[1].wait_recv()
    transpose(in_two, turned, 0, theirs_begin, own_tokens // TILE)
    two_turned = pltpu.make_async_copy(turned, in_two_t, t_sem.at[1])
    two_turned.start()
    for unit in list(ffn_units)[1:]:
        gather.step(unit, 4)
    for index in range(QUARTERS // 2, QUARTERS):
        cot_swap(index, arrival=True).wait_recv()
    transpose(cots, turned_cot, 0, theirs_begin + own_tokens // 2, own_tokens // TILE // 2)
    cot_copies = [
        pltpu.make_async_copy(cots, cot_all, t_sem.at[2]),
        pltpu.make_async_copy(turned_cot, cot_t, t_sem.at[3]),
    ]
    for copy in cot_copies:
        copy.start()
    for unit in ffn_units:
        gather.step(unit, 5)
    for unit in ffn_units:
        gather.end(unit)
    for unit in range(units + 1):
        gather.sent(unit)
    hid_swap[0].wait_send()
    mix_swap.wait_send()
    two_swap[0].wait_send()
    for index in range(QUARTERS):
        cot_swap(index).wait_send()
    for copy in [wa_out, two_turned] + cot_copies:
        copy.wait()


def forward_attention(hidden_in, cotangent, vectors, weights, heads):
    own_tokens, width = hidden_in.shape
    tokens = 2 * own_tokens
    rows = weights[0].shape[0]
    chunks = -(-weights[4].shape[1] // CHUNK)
    units = (chunks - LATER) // PAIRS
    early = units * PAIRS
    width_q = heads * HD
    width_attn = 2 * width_q + 2 * HD
    wide = 3 * CHUNK
    vmem = pl.BlockSpec(memory_space=pltpu.VMEM)
    hbm = pl.BlockSpec(memory_space=pl.ANY)
    dma = pltpu.SemaphoreType.DMA
    shape = jax.ShapeDtypeStruct
    pieces = 2 * HALF + 1
    return pl.pallas_call(
        functools.partial(forward_kernel, (rows, heads, units)),
        in_specs=[vmem, hbm] + [vmem] * 7 + [hbm] * 7,
        out_specs=[hbm, hbm, vmem, hbm, hbm] + [vmem] * 10 + [hbm, hbm],
        out_shape=[
            shape((early, width, wide), BF16),
            shape((width, width_attn), BF16),
            shape((tokens, width), BF16),
            shape((tokens, width), BF16),
            shape((width, tokens), BF16),
            shape((tokens, width_q), BF16),
            shape((tokens, HD), BF16),
            shape((tokens, HD), BF16),
            shape((tokens, width_q), BF16),
            shape((heads, 8, tokens), F32),
            shape((own_tokens, width), F32),
            shape((tokens, width), BF16),
            shape((1, width_q + 2 * HD + 2 * width + tokens), F32),
            shape((tokens, HD), F32),
            shape((tokens, HD), F32),
            shape((width, tokens), BF16),
            shape((width, tokens), BF16),
        ],
        scratch_shapes=[
            pltpu.VMEM((width, width_attn), BF16),
            pltpu.VMEM((tokens, width_q + 2 * HD), F32),
            pltpu.VMEM((own_tokens, width), BF16),
            pltpu.VMEM((own_tokens, width), BF16),
            pltpu.VMEM((early, rows, wide), BF16),
            pltpu.VMEM((units, 2 * HALF - 1, PAIRS, rows, wide), BF16),
            pltpu.VMEM((tokens, width), BF16),
            pltpu.VMEM((tokens, width), BF16),
            pltpu.VMEM((width, tokens), BF16),
            pltpu.VMEM((width, tokens), BF16),
            dma((7,)), dma((early, 3)), dma((units + 1, pieces)),
            dma((units + 1, HALF, 2)), dma((units + 1, HALF, 2)),
            dma((units + 1, pieces)), dma((units + 1, pieces)),
            dma((3 + QUARTERS,)), dma((3 + QUARTERS,)), dma((4,)),
        ],
        compiler_params=pltpu.CompilerParams(
            collective_id=1, has_side_effects=True, vmem_limit_bytes=63 * 2**20
        ),
        cost_estimate=pl.CostEstimate(
            flops=6 * tokens * width * width_attn, bytes_accessed=120 * 2**20, transcendentals=0
        ),
        name="forward_attention",
    )(hidden_in, cotangent, *vectors, *weights)


class Sums:
    def __init__(self, here, own, places, send_sem, recv_sem):
        self.here, self.own, self.places = here, own, places
        self.send_sem, self.recv_sem = send_sem, recv_sem

    def chip(self, step, way):
        distance = HALF - step
        return self.here.chip(distance if way == 0 else CHIPS - distance)

    def copy(self, o, p, step, way, m, columns):
        here, rows = self.here, self.here.rows
        return pltpu.make_async_remote_copy(
            src_ref=self.own.at[o, here.part(self.chip(step, way), way if step == 0 else None), columns],
            dst_ref=self.places.at[p, step, way, 0 : rows // 2 if step == 0 else rows, columns],
            send_sem=self.send_sem.at[p, step, way, m],
            recv_sem=self.recv_sem.at[p, step, way, m],
            device_id={"dp": here.next[way]},
            device_id_type=MESH,
        )

    def columns(self, pieces, m):
        count, size = pieces
        return pl.ds(pl.multiple_of(m * size, HD), size)

    def start(self, o, p, pieces):
        @pl.loop(0, pieces[0])
        def _(m):
            for way in range(2):
                self.copy(o, p, 0, way, m, self.columns(pieces, m)).start()

    def step(self, o, p, step, pieces):
        here, own = self.here, self.own

        @pl.loop(0, pieces[0])
        def _(m):
            columns = self.columns(pieces, m)
            for way in range(2):
                self.copy(o, p, step - 1, way, m, columns).wait()
            for way in range(2):
                part = here.part(self.chip(step, way), way if step == 1 else None)
                size = here.rows // 2 if step == 1 else here.rows
                own[o, part, columns] = (
                    own[o, part, columns].astype(F32)
                    + self.places[p, step - 1, way, 0:size, columns].astype(F32)
                ).astype(BF16)
                self.copy(o, p, step, way, m, columns).start()

    def end(self, o, p, pieces, target):
        own, last = self.own, HALF - 1
        part = self.here.part(self.here.chip(0))

        @pl.loop(0, pieces[0])
        def _(m):
            columns = self.columns(pieces, m)
            for way in range(2):
                self.copy(o, p, last, way, m, columns).wait()
            target[:, columns] = (
                own[o, part, columns].astype(F32)
                + self.places[p, last, 0, :, columns].astype(F32)
                + self.places[p, last, 1, :, columns].astype(F32)
            )


EVENTS = {
    (0, "a"): "G11 G21",
    (0, "c"): "G02",
    (0, "f"): "G12",
    (1, "a"): "R00",
    (1, "b"): "G22",
    (1, "e"): "G03",
    (2, "a"): "R10",
    (2, "b"): "G13",
    (2, "c"): "R01 G23",
    (3, "a"): "G04 R11",
    (3, "c"): "G14",
    (4, "a"): "R02",
    (4, "b"): "G24",
    (4, "c"): "G05",
    (4, "e"): "R12",
    (4, "f"): "G15",
    (5, "a"): "R03 R20",
    (5, "c"): "G25 R13",
    (6, "0a"): "R04 R21",
    (6, "1a"): "R14 R22",
    (6, "1b"): "R30",
    (6, "2b"): "R23",
    (7, "0a"): "R31",
    (7, "1a"): "R24 R32 R40",
    (7, "2a"): "R33",
    (7, "2b"): "R41",
    (8, "1a"): "R34 R42",
    (8, "1b"): "R43",
    (8, "2b"): "R44",
}
SETS = 3


def ffn_kernel(
    cfg, in2_hbm, cot_hbm, in2t_hbm, cott_hbm, w_ffn, w_attn, wg, wu, wd,
    hiddens, gin_own, later, grad_g, grad_u, grad_d, w_other, w_late,
    in2, cot, in2t, cott, wbuf, acts, gin, own, sent, sib, ring, stage, pack,
    in_sem, w_sem, sib_send, sib_recv, ring_send, ring_recv, out_sem, g_sem, end_sem, free_sem,
    pack_sem, store_sem, hop_send, hop_recv, side_send, side_recv, park_sem, fetch_sem, hid_sem,
):
    rows, chunks, total = cfg
    grads = (grad_g, grad_u, grad_d)
    tokens, width = in2.shape
    side_rows = CHIPS * rows
    own_tokens = tokens // 2
    first = chunks - LATER
    rings = first - 1
    here = Spot(rows)
    shard = here.shard
    sums = Sums(here, own, ring, ring_send, ring_recv)
    ring_pieces = (3, CHUNK)
    own_rows = pl.ds(pl.multiple_of(shard * own_tokens, TILE), own_tokens)
    other_rows = pl.ds(pl.multiple_of((1 - shard) * own_tokens, TILE), own_tokens)

    def load(chunk, m):
        columns = (slice(0, 2 * CHUNK), slice(2 * CHUNK, 3 * CHUNK))[m]
        return pltpu.make_async_copy(
            w_ffn.at[chunk, :, columns], wbuf.at[:, columns], w_sem.at[m]
        )

    def size_of(i):
        return units_of(first + i, total)

    def load_late(i, m):
        size = size_of(i)
        columns = (slice(0, 2 * size), slice(2 * size, 3 * size))[m]
        return pltpu.make_async_copy(
            w_late.at[i, :, columns], wbuf.at[:, columns], w_sem.at[m]
        )

    def home(unit, member, half):
        return w_late.at[unit, here.part(member, half), 0 : 3 * size_of(unit)]

    def held(unit, step, way, half):
        size = rows if half is None else rows // 2
        columns = slice(0, 3 * size_of(unit))
        if step == 0:
            return pack.at[unit, :, columns]
        slot = 2 * (step - 1) + way
        whole = 2 * HALF - 2
        if unit < 2:
            buffer, begin = 1 + unit, (whole if step == HALF else slot) * rows
            offset = 0
            if half is not None:
                offset = half * size
        else:
            base = (whole + 1) * rows
            if step == HALF:
                buffer, begin, offset = 1 + way, base + whole // 2 * rows, 0
            else:
                buffer, begin = 1 + slot // (whole // 2), base + slot % (whole // 2) * rows
                offset = 0 if half is None else half * size
        return acts.at[buffer, begin + offset : begin + offset + size, columns]

    gather = Gather(
        here, held, home, lambda unit: False, hop_send, hop_recv, side_send, side_recv, store_sem
    )
    own_blocks = pack_copies((wg, wu, wd), pack, range(first, chunks), pack_sem)

    inputs = [
        pltpu.make_async_copy(in2_hbm, in2, in_sem.at[0]),
        pltpu.make_async_copy(cot_hbm, cot, in_sem.at[1]),
    ]
    turned = []
    for i, (source, target) in enumerate(((in2t_hbm, in2t), (cott_hbm, cott))):
        for side in range(2):
            for chip in range(CHIPS):
                member = 2 * chip + (here.core if side == 0 else 1 - here.core)
                begin = side * side_rows + chip * rows
                turned.append(pltpu.make_async_copy(
                    source.at[here.part(member), :], target.at[begin : begin + rows, :],
                    in_sem.at[2 + i],
                ))
    for copy in own_blocks + [load(0, m) for m in range(2)] + inputs:
        copy.start()
    here.greet()
    for copy in own_blocks:
        copy.wait()
    gather.start(0)

    def result_copies(chunk):
        return [
            pltpu.make_async_copy(
                stage.at[:, m * CHUNK : (m + 1) * CHUNK],
                grads[m].at[:, tile_of(chunk, CHUNK)],
                out_sem.at[m],
            )
            for m in range(3)
        ]

    def fetch(chunk):
        return pltpu.make_async_copy(
            later.at[chunk - SETS], own.at[chunk % SETS], fetch_sem.at[chunk % SETS]
        )

    def park(chunk, p, early, size=CHUNK):
        columns = slice(0, 3 * size)
        target = own.at[chunk] if early else later.at[chunk - SETS, :, columns]
        return pltpu.make_async_copy(sib.at[p, :, columns], target, park_sem.at[p])

    def ring_event(chunk, step):
        o, p = chunk % SETS, chunk % 2
        if step == 0:
            if chunk >= SETS:
                fetch(chunk).wait()
            sums.start(o, p, ring_pieces)
        elif step < HALF:
            sums.step(o, p, step, ring_pieces)
        else:
            if chunk:
                for copy in result_copies(chunk - 1):
                    copy.wait()
            sums.end(o, p, ring_pieces, stage)
            for copy in result_copies(chunk):
                copy.start()
            if chunk + SETS < rings:
                fetch(chunk + SETS).start()

    def run(events):
        for event in events.split():
            index, step = int(event[1]), int(event[2])
            if event[0] == "R":
                ring_event(index, step)
            elif step == 1:
                gather.start(index)
            else:
                gather.step(index, step)

    def sib_copy(p, m, size):
        columns = slice(m * size, (m + 1) * size)
        return pltpu.make_async_remote_copy(
            src_ref=sent.at[:, columns],
            dst_ref=sib.at[p, :, columns],
            send_sem=sib_send.at[m],
            recv_sem=sib_recv.at[p, m],
            device_id={"dp": here.sibling},
            device_id_type=MESH,
        )

    def weight_copy():
        return pltpu.make_async_remote_copy(
            src_ref=w_attn.at[:, 0 : w_other.shape[1]], dst_ref=w_other,
            send_sem=g_sem.at[2], recv_sem=g_sem.at[3],
            device_id={"mp": 1 - shard}, device_id_type=MESH,
        )

    def gin_copy():
        return pltpu.make_async_remote_copy(
            src_ref=in2.at[other_rows, :], dst_ref=cot.at[own_rows, :],
            send_sem=g_sem.at[0], recv_sem=g_sem.at[1],
            device_id={"mp": 1 - shard}, device_id_type=MESH,
        )

    def hidden_copy(index, chunk, size=CHUNK):
        return pltpu.make_async_copy(
            acts.at[index, :, 2 * size : 3 * size], hiddens.at[chunk, :, 0:size], hid_sem.at[index]
        )

    def forward(index, part, size=CHUNK):
        for begin in range(0, size, TILE):
            stop = min(begin + TILE, size)
            gates, ups, downs = (slice(m * size + begin, m * size + stop) for m in range(3))
            gate = contract(in2[part, :], wbuf[:, gates], 1, 0)
            up = contract(in2[part, :], wbuf[:, ups], 1, 0)
            grad = contract(cot[part, :], wbuf[:, downs], 1, 0)
            sig = 0.5 * jnp.tanh(0.5 * gate) + 0.5
            swish = gate * sig
            acts[index, part, downs] = (swish * up).astype(BF16)
            acts[index, part, gates] = (grad * up * (sig + swish - swish * sig)).astype(BF16)
            acts[index, part, ups] = (grad * swish).astype(BF16)

    def back_gin(index, part, size=CHUNK):
        @pl.loop(0, width // TILE)
        def _(n):
            gin[part, tile_of(n)] += contract(
                acts[index, part, 0 : 2 * size], wbuf[tile_of(n), 0 : 2 * size], 1, 1
            )

    def weight_grads(index, p, between, size=CHUNK):
        for m, left in enumerate((in2t, in2t, cott)):
            columns = slice(m * size, (m + 1) * size)
            sent[:, columns] = contract(
                left[side_rows:, :], acts[index, :, columns], 1, 0
            ).astype(BF16)
            sib_copy(p, m, size).start()
        between()
        for m, left in enumerate((in2t, in2t, cott)):
            columns = slice(m * size, (m + 1) * size)
            sib_copy(p, m, size).wait()
            sib[p, :, columns] = (
                contract(left[0:side_rows, :], acts[index, :, columns], 1, 0)
                + sib[p, :, columns].astype(F32)
            ).astype(BF16)

    gin[...] = jnp.zeros_like(gin)
    for copy in inputs:
        copy.wait()
    for copy in turned:
        copy.start()

    def at_point(j, point):
        for chunk in range(first):
            if (chunk, point) in EVENTS:
                @pl.when(j == chunk)
                def _():
                    run(EVENTS[chunk, point])

    weight_copy().start()

    @pl.loop(0, first)
    def _(j):
        p = lax.rem(j, 2)
        for m in range(2):
            load(j, m).wait()

        @pl.when(j >= 1)
        def _():
            hidden_copy(0, j - 1).wait()

        forward(0, slice(0, own_tokens))

        @pl.when((j >= 1) & (j <= SETS))
        def _():
            park(j - 1, 1 - p, True).wait()

        @pl.when(j > SETS)
        def _():
            park(j - 1, 1 - p, False).wait()

        at_point(j, "a")
        forward(0, slice(own_tokens, tokens))
        hidden_copy(0, j).start()
        at_point(j, "b")

        @pl.when(j == first - 1)
        def _():
            gather.end(0)
            gather.sent(0)

        @pl.when(j + 1 < first)
        def _():
            load(j + 1, 1).start()

        @pl.when(j == first - 1)
        def _():
            load_late(0, 1).start()

        back_gin(0, slice(0, tokens))

        @pl.when(j + 1 < first)
        def _():
            load(j + 1, 0).start()

        @pl.when(j == first - 1)
        def _():
            load_late(0, 0).start()

        at_point(j, "c")

        @pl.when(j == 0)
        def _():
            for i, ref in enumerate((in2t, cott)):
                pltpu.make_async_copy(ref, ref, in_sem.at[2 + i]).wait()

        weight_grads(0, p, lambda: at_point(j, "e"))

        @pl.when(j < SETS)
        def _():
            park(j, p, True).start()

        @pl.when(j >= SETS)
        def _():
            park(j, p, False).start()

        at_point(j, "f")

    hidden_copy(0, first - 1).wait()
    for unit in range(1, LATER):
        gather.end(unit)
        gather.sent(unit)

    for half in range(2):
        part = (other_rows, own_rows)[half]
        for i in range(LATER):
            size = size_of(i)
            for m in range(2):
                load_late(i, m).wait()
            forward(i, part, size)
            if half == 1:
                hidden_copy(i, first + i, size).start()
            run(EVENTS.get((first + half, f"{i}a"), ""))
            following = i + 1 if i + 1 < LATER else 0
            same = size_of(following) == size
            more = half == 0 or i + 1 < LATER
            if more and same:
                load_late(following, 1).start()
            back_gin(i, part, size)
            if more:
                load_late(following, 0).start()
            if more and not same:
                load_late(following, 1).start()
            run(EVENTS.get((first + half, f"{i}b"), ""))
        if half == 0:
            pl.semaphore_signal(
                free_sem, inc=1, device_id={"mp": 1 - shard}, device_id_type=MESH
            )

            @pl.loop(0, own_tokens // TILE)
            def _(t):
                of = pl.ds(pl.multiple_of((1 - shard) * own_tokens + t * TILE, TILE), TILE)
                in2[of, :] = gin[of, :].astype(BF16)

            pl.semaphore_wait(free_sem, 1)
            gin_copy().start()

    for i in range(LATER):
        chunk, size = first + i, size_of(i)
        p = chunk % 2
        park(chunk - 1, 1 - p, False).wait()
        weight_grads(i, p, lambda: run(EVENTS.get((first + 2, f"{i}a"), "")), size)
        park(chunk, p, False, size).start()
        run(EVENTS.get((first + 2, f"{i}b"), ""))
    gin_copy().wait()

    @pl.loop(0, own_tokens // TILE)
    def _(t):
        of = pl.ds(pl.multiple_of(shard * own_tokens + t * TILE, TILE), TILE)
        at = pl.ds(pl.multiple_of((1 - shard) * own_tokens + t * TILE, TILE), TILE)
        gin[of, :] = gin[of, :] + cot[at, :].astype(F32)

    gin_out = pltpu.make_async_copy(gin.at[own_rows, :], gin_own, end_sem.at[0])
    gin_out.start()
    weight_copy().wait()
    last_park = park(chunks - 1, (chunks - 1) % 2, False, size_of(LATER - 1))
    for copy in [gin_out, last_park] + result_copies(rings - 1):
        copy.wait()
    for i in range(LATER):
        hidden_copy(i, first + i, size_of(i)).wait()


def feed_forward(inputs_two, grad_ffn, in_two_t, cot_t, w_ffn, w_attn, width_qkv, weights):
    tokens, width = inputs_two.shape
    rows = weights[0].shape[0]
    chunks = w_ffn.shape[0] + LATER
    pieces = 2 * HALF + 1
    hbm = pl.BlockSpec(memory_space=pl.ANY)
    side_rows, wide = CHIPS * rows, 3 * CHUNK
    dma = pltpu.SemaphoreType.DMA
    shape = jax.ShapeDtypeStruct
    half = (tokens // 2, width)
    return pl.pallas_call(
        functools.partial(ffn_kernel, (rows, chunks, weights[0].shape[1])),
        in_specs=[hbm] * 9,
        out_specs=[hbm] * 8,
        out_shape=[
            shape((chunks, tokens, CHUNK), BF16), shape(half, F32),
            shape((chunks - SETS, side_rows, wide), BF16),
        ] + [shape((rows, (chunks - LATER - 1) * CHUNK), F32)] * 3 + [
            shape((width, width_qkv), BF16),
            shape((LATER, width, wide), BF16),
        ],
        scratch_shapes=[
            pltpu.VMEM((tokens, width), BF16),
            pltpu.VMEM((tokens, width), BF16),
            pltpu.VMEM((width, tokens), BF16),
            pltpu.VMEM((width, tokens), BF16),
            pltpu.VMEM((width, wide), BF16),
            pltpu.VMEM((LATER, tokens, wide), BF16),
            pltpu.VMEM((tokens, width), F32),
            pltpu.VMEM((SETS, side_rows, wide), BF16),
            pltpu.VMEM((side_rows, wide), BF16),
            pltpu.VMEM((2, side_rows, wide), BF16),
            pltpu.VMEM((2, HALF, 2, rows, wide), BF16),
            pltpu.VMEM((rows, wide), F32),
            pltpu.VMEM((LATER, rows, wide), BF16),
            dma((4,)), dma((2,)), dma((3,)), dma((2, 3)),
            dma((2, HALF, 2, 3)), dma((2, HALF, 2, 3)), dma((3,)), dma((4,)), dma((1,)),
            pltpu.SemaphoreType.REGULAR,
            dma((LATER, 3)), dma((LATER, pieces)), dma((LATER, HALF, 2)), dma((LATER, HALF, 2)),
            dma((LATER, pieces)), dma((LATER, pieces)), dma((2,)), dma((SETS,)), dma((LATER,)),
        ],
        compiler_params=pltpu.CompilerParams(
            collective_id=2, has_side_effects=True, vmem_limit_bytes=63 * 2**20
        ),
        cost_estimate=pl.CostEstimate(
            flops=18 * tokens * width * chunks * CHUNK, bytes_accessed=80 * 2**20,
            transcendentals=tokens * chunks * CHUNK,
        ),
        name="feed_forward",
    )(inputs_two, grad_ffn, in_two_t, cot_t, w_ffn, w_attn, *weights)


JOBS = 1 + LATER


BACK_EVENTS = {
    "w0": "01 11",
    "w1": "20",
    "w2": "02",
    "w4": "12",
    "w6": "21",
    "w8": "03",
    "w9": "13",
    "h0": "22",
    "h3": "04",
    "h4": "30",
    "h5": "14",
    "o": "23 31",
    "q1": "40",
    "t1": "24",
    "t2": "32",
    "t3": "41",
    "g": "33",
    "b": "42",
    "u1": "50 34 43",
    "l0": "51",
    "l2": "44 52 53",
    "z1": "54",
}


def backward_kernel(
    cfg, later, gin_hbm, middle_hbm, cot_hbm, hiddens, w_ffn, w_late, w_other, w_attn, qrot_hbm, krot_hbm,
    vlow_hbm, lse_hbm, mixed_hbm, in_one_t, hid_hbm, cos_ref, sin_ref, vec_ref,
    layer_out, grad_input, small_out, grad_g, grad_u, grad_d, grad_qkv, grad_out, kept,
    own, ring, sent, sib, lefts, gin, middle, tall, wa, qrot, krot, vlow, lse, mixed,
    gmix, dqkv, gk, gv, osend, orecv, cots, got, stage, small, small_got,
    in_sem, ring_send, ring_recv, sib_send, sib_recv, x_send, x_recv, out_sem, s_send, s_recv, down_sem, hid_sem,
):
    rows, heads, skip, tail = cfg
    grads = (grad_g, grad_u, grad_d)
    own_tokens, width = gin.shape
    tokens = 2 * own_tokens
    width_q = heads * HD
    width_qkv = width_q + 2 * HD
    side_rows = CHIPS * rows
    _, gain_one, gain_two, start_of = small_inputs(vec_ref, width_qkv, width)
    here = Spot(rows)
    shard, me = here.shard, here.me
    sums = Sums(here, own, ring, ring_send, ring_recv)
    wide_qkv, wide_out = (2, width_qkv // 2), (2, width_q // 2)
    pieces = [(3, CHUNK)] * (JOBS - 1) + [(3, tail), wide_qkv, wide_out]
    own_rows = pl.ds(pl.multiple_of(shard * own_tokens, TILE), own_tokens)
    other_rows = pl.ds(pl.multiple_of((1 - shard) * own_tokens, TILE), own_tokens)

    def at_own(t, size=TILE):
        return pl.ds(pl.multiple_of(shard * own_tokens + t * size, size), size)

    def at_other(t, size=TILE):
        return pl.ds(pl.multiple_of((1 - shard) * own_tokens + t * size, size), size)

    def get(index, source, target):
        return pltpu.make_async_copy(source, target, in_sem.at[index])

    sums_in = [get(i, later.at[skip + i], own.at[i]) for i in range(3)]
    norm_in = [get(3, gin_hbm, gin), get(4, middle_hbm, middle), get(5, cot_hbm, cots)]
    rest_in = [
        get(7, w_attn, wa), get(8, qrot_hbm, qrot), get(9, krot_hbm, krot), get(10, vlow_hbm, vlow),
        get(11, lse_hbm, lse), get(12, mixed_hbm, mixed),
    ]
    for copy in sums_in[:2] + norm_in + sums_in[2:] + rest_in:
        copy.start()
    for side in range(2):
        for chip in range(CHIPS):
            member = 2 * chip + (here.core if side == 0 else 1 - here.core)
            begin = side * side_rows + chip * rows
            get(13, in_one_t.at[here.part(member), :], lefts.at[0, begin : begin + rows, :]).start()

    def bit(value):
        return lax.rem(lax.div(me, value), 2)

    def flipped(*values):
        return me + sum(value - 2 * value * bit(value) for value in values)

    ranks = (here.core + 2 * shard, bit(2) + 2 * bit(4), bit(8))
    partners = (
        ({"dp": flipped(1)}, {"mp": 1 - shard}, {"dp": flipped(1), "mp": 1 - shard}),
        ({"dp": flipped(2)}, {"dp": flipped(4)}, {"dp": flipped(2, 4)}),
        ({"dp": flipped(8)},),
    )

    def rank_of(group, k):
        rank = ranks[group]
        return (rank + 1 - 2 * lax.rem(rank, 2), rank + 2 - 4 * lax.div(rank, 2), 3 - rank)[k]

    barrier = pltpu.get_barrier_semaphore()
    greeted = [p for group in partners for p in group] + [{"dp": n} for n in here.next]
    for target in greeted:
        pl.semaphore_signal(barrier, inc=1, device_id=target, device_id_type=MESH)
    pl.semaphore_wait(barrier, len(greeted))

    def swap_copy(index, src, dst):
        return pltpu.make_async_remote_copy(
            src_ref=src, dst_ref=dst, send_sem=x_send.at[index], recv_sem=x_recv.at[index],
            device_id={"mp": 1 - shard}, device_id_type=MESH,
        )

    some = own_tokens // 2

    def out_swap(index):
        part = slice(index * some, (index + 1) * some)
        return swap_copy(index, osend.at[part, :], orecv.at[part, :])

    half_tiles = own_tokens // TILE

    def attn_swap(t):
        return swap_copy(2 + t, tall.at[at_own(t), :], tall.at[at_own(t), :])

    def attn_got(t):
        return swap_copy(2 + t, tall.at[at_other(t), :], tall.at[at_other(t), :])

    one_swap = swap_copy(2 + half_tiles, dqkv.at[other_rows, :], got)

    def result_copies(job):
        if job < JOBS:
            count, size = pieces[job]
            return [
                pltpu.make_async_copy(
                    stage.at[:, m * size : (m + 1) * size],
                    grads[m].at[:, job * CHUNK : job * CHUNK + size], out_sem.at[m],
                )
                for m in range(count)
            ]
        target = (grad_qkv, grad_out)[job - JOBS]
        return [pltpu.make_async_copy(stage.at[:, 0 : target.shape[1]], target, out_sem.at[0])]

    last_in = get(0, later.at[skip + 3, :, 0 : 3 * tail], own.at[0, :, 0 : 3 * tail])

    def run(point):
        for event in BACK_EVENTS.get(point, "").split():
            job, step = int(event[0]), int(event[1])
            o = p = job % 3
            if step == 0:
                if job == 2:
                    sums_in[2].wait()
                if job == 3:
                    last_in.wait()
                sums.start(o, p, pieces[job])
            elif step < HALF:
                sums.step(o, p, step, pieces[job])
            else:
                if job:
                    for copy in result_copies(job - 1):
                        copy.wait()
                sums.end(o, p, pieces[job], stage)
                for copy in result_copies(job):
                    copy.start()
                if job == 0:
                    last_in.start()

    for i in range(2):
        sums_in[i].wait()
        sums.start(i, i, pieces[i])

    for copy in norm_in:
        copy.wait()
    small[0, :, :] = jnp.zeros_like(small[0])

    @pl.loop(0, half_tiles)
    def _(t):
        part = tile_of(t)
        v = middle[part, :]
        factor = lax.rsqrt(jnp.mean(v * v, axis=-1, keepdims=True) + EPS)
        unit = v * factor
        e = gin[part, :]
        scaled = e * gain_two
        inner = jnp.mean(scaled * unit, axis=-1, keepdims=True)
        total = cots[part, :].astype(F32) + factor * (scaled - unit * inner)
        middle[part, :] = total
        gin[part, :] = v
        tall[at_own(t), :] = total.astype(BF16)
        attn_swap(t).start()
        small[0, 1:2, :] += jnp.sum(e * unit, axis=0, keepdims=True)

    keep = pltpu.make_async_copy(middle, kept, out_sem.at[5])
    keep.start()
    keep.wait()
    middle[...] = jnp.zeros_like(middle)
    early = w_ffn.shape[0]
    chunks = early + w_late.shape[0]

    def down_in(chunk):
        size = CHUNK if chunk + 1 < chunks else tail
        slot = chunk % 2 * CHUNK
        source = w_ffn.at[chunk] if chunk < early else w_late.at[chunk - early]
        return [
            pltpu.make_async_copy(
                source.at[:, 2 * size : 3 * size], lefts.at[1, :, slot : slot + size],
                down_sem.at[chunk % 2],
            ),
            pltpu.make_async_copy(
                hiddens.at[chunk, :, 0:size], dqkv.at[:, slot : slot + size], hid_sem.at[chunk % 2]
            ),
        ]

    for copy in down_in(0):
        copy.start()
    for chunk in range(chunks):
        if chunk + 1 < chunks:
            for copy in down_in(chunk + 1):
                copy.start()
        for copy in down_in(chunk):
            copy.wait()
        begin = chunk % 2 * CHUNK
        columns = slice(begin, begin + (CHUNK if chunk + 1 < chunks else tail))

        @pl.loop(0, width // TILE)
        def _(n):
            weight = lefts[1, tile_of(n), columns]
            middle[:, tile_of(n)] += contract(dqkv[other_rows, columns], weight, 1, 1)
            gin[:, tile_of(n)] += contract(dqkv[own_rows, columns], weight, 1, 1)

        run(f"w{chunk}")

    osend[...] = middle[...].astype(BF16)
    out_swap(0).start()
    run("w9")

    for copy in rest_in:
        copy.wait()
    for t in range(half_tiles):
        attn_got(t).wait_recv()

    @pl.loop(0, tokens // TILE)
    def _(t):
        gmix[tile_of(t), :] = contract(tall[tile_of(t), :], wa[:, width_qkv:], 1, 0).astype(BF16)

    gk[...] = jnp.zeros_like(gk)
    gv[...] = jnp.zeros_like(gv)

    @pl.loop(0, heads)
    def _(h):
        columns = tile_of(h, HD)
        for i in range(SEQ_LEN // BLOCK):
            low, high = key_range(i)
            part = pl.ds(i * BLOCK, BLOCK)
            query, grad = qrot[part, columns], gmix[part, columns]
            keys = krot[low:high, :]
            scores = contract(keys, query, 1, 1) * SCALE
            seen = visible_keys(start_of(i), low, high, i)
            probs = jnp.where(seen, jnp.exp(scores - lse[h, 0:1, part]), 0.0)
            grad_probs = contract(vlow[low:high, :], grad, 1, 1)
            row_term = jnp.sum(probs * grad_probs, axis=0, keepdims=True)
            grad_scores = (probs * (grad_probs - row_term)).astype(BF16)
            gk[low:high, :] += contract(grad_scores, query, 1, 0)
            gv[low:high, :] += contract(probs.astype(BF16), grad, 1, 0)
            dqkv[part, columns] = turn(
                contract(grad_scores, keys, 0, 0) * SCALE, cos_ref[part, :], -sin_ref[part, :]
            ).astype(BF16)

        for head in range(heads):
            if f"h{head}" in BACK_EVENTS:
                @pl.when(h == head)
                def _():
                    run(f"h{head}")

    dqkv[:, width_q : width_q + HD] = turn(gk[...] * SCALE, cos_ref[...], -sin_ref[...]).astype(BF16)
    dqkv[:, width_q + HD :] = gv[...].astype(BF16)

    one_swap.start()
    out_swap(1).start()
    run("o")

    side_sent = (sent, gmix.at[0:side_rows, :])
    side_got = (sib, qrot.at[0:side_rows, :])

    def side_copy(job, m, columns):
        return pltpu.make_async_remote_copy(
            src_ref=side_sent[job].at[:, columns],
            dst_ref=side_got[job].at[:, columns],
            send_sem=sib_send.at[job, m],
            recv_sem=sib_recv.at[job, m],
            device_id={"dp": here.sibling},
            device_id_type=MESH,
        )

    get(13, lefts.at[0], lefts.at[0]).wait()

    def send_side(job, left, right, pieces):
        for m in range(pieces[0]):
            columns = slice(m * pieces[1], (m + 1) * pieces[1])
            side_sent[job][:, columns] = contract(
                lefts[left, side_rows:, :], right[:, columns], 1, 0
            ).astype(BF16)
            side_copy(job, m, columns).start()

    def own_side(job, left, right, pieces, o):
        for m in range(pieces[0]):
            columns = slice(m * pieces[1], (m + 1) * pieces[1])
            side_copy(job, m, columns).wait()
            own[o, :, columns] = (
                contract(lefts[left, 0:side_rows, :], right[:, columns], 1, 0)
                + side_got[job][:, columns].astype(F32)
            ).astype(BF16)

    send_side(0, 0, dqkv, wide_qkv)
    run("q0")
    own_side(0, 0, dqkv, wide_qkv, 1)
    other_in = get(6, w_other, lefts.at[0])
    other_in.start()
    run("q1")

    for group in range(width // (4 * rows)):
        @pl.loop(0, tokens // TILE)
        def _(t):
            part = tile_of(t)
            turned = tall[part, group * 4 * rows : (group + 1) * 4 * rows].T
            for k in range(4):
                chip, odd = (4 * group + k) // 2, k % 2
                side = odd + here.core - 2 * odd * here.core
                to = pl.ds(pl.multiple_of(side * side_rows + chip * rows, 16), rows)
                lefts[1, to, part] = turned[k * rows : (k + 1) * rows, :]

        run(f"t{group}")

    for t in range(half_tiles):
        attn_swap(t).wait_send()
    hid_in = get(15, hid_hbm, tall)
    hid_in.start()

    fac = gk
    hid_in.wait()

    @pl.loop(0, tokens // TILE)
    def _(t):
        v = tall[tile_of(t), :].astype(F32)
        factor = lax.rsqrt(jnp.mean(v * v, axis=-1, keepdims=True) + EPS)
        fac[tile_of(t), :] = jnp.broadcast_to(factor, (TILE, HD))

    run("f")

    @pl.loop(0, width // TILE)
    def _(n):
        e = contract(dqkv[other_rows, :], wa[tile_of(n), 0:width_qkv], 1, 1)
        unit = tall[other_rows, tile_of(n)].astype(F32) * fac[other_rows, 0:1]
        small[0, 0:1, tile_of(n)] += jnp.sum(e * unit, axis=0, keepdims=True)

    run("g")

    @pl.loop(0, width // TILE)
    def _(n):
        e = contract(dqkv[own_rows, :], wa[tile_of(n), 0:width_qkv], 1, 1)
        middle[:, tile_of(n)] = e
        unit = tall[own_rows, tile_of(n)].astype(F32) * fac[own_rows, 0:1]
        small[0, 0:1, tile_of(n)] += jnp.sum(e * unit, axis=0, keepdims=True)

    @pl.loop(0, tokens // TILE)
    def _(t):
        bias = jnp.sum(dqkv[tile_of(t), :].astype(F32), axis=0, keepdims=True)
        at_query = pl.ds(pl.multiple_of(shard * width_q, HD), width_q)
        small[0, 2:3, at_query] += bias[:, 0:width_q]
        small[0, 3:4, tile_of(shard, HD)] += bias[:, width_q : width_q + HD]
        small[0, 3:4, tile_of(shard + 2, HD)] += bias[:, width_q + HD :]

    run("b")

    def small_copy(group, k):
        return pltpu.make_async_remote_copy(
            src_ref=small.at[group], dst_ref=small_got.at[group, ranks[group]],
            send_sem=s_send.at[group, k], recv_sem=s_recv.at[group, ranks[group]],
            device_id=partners[group][k], device_id_type=MESH,
        )

    def small_start(group):
        for k in range(len(partners[group])):
            small_copy(group, k).start()
        small_got[group, ranks[group]] = small[group]

    def small_end(group):
        count = len(partners[group])
        for k in range(count):
            ref = small_got.at[group, rank_of(group, k)]
            pltpu.make_async_remote_copy(
                src_ref=ref, dst_ref=ref, send_sem=s_send.at[group, k],
                recv_sem=s_recv.at[group, rank_of(group, k)],
                device_id=partners[group][k], device_id_type=MESH,
            ).wait_recv()
            small_copy(group, k).wait_send()
        total = small_got[group, 0]
        for rank in range(1, count + 1):
            total = total + small_got[group, rank]
        small[group + 1] = total

    small_start(0)
    send_side(1, 1, mixed, wide_out)
    run("u0")
    own_side(1, 1, mixed, wide_out, 2)
    small_end(0)
    small_start(1)
    run("u1")

    def layer_rows(index):
        part = slice(index * some, (index + 1) * some)
        out_swap(index).wait()
        orecv[part, :] = (gin[part, :] + orecv[part, :].astype(F32)).astype(BF16)
        copy = pltpu.make_async_copy(
            orecv.at[part, :], layer_out.at[part, :], out_sem.at[(3, 6)[index]]
        )
        copy.start()
        return copy

    def keep_in(index):
        part = slice(index * some, (index + 1) * some)
        return get(14, kept.at[part, :], gin.at[0:some, :])

    layer_copies = [layer_rows(0)]
    keep_in(0).start()
    run("l0")
    small_end(1)
    small_start(2)
    run("l1")
    small_end(2)
    run("l2")
    small_out[...] = small[3]

    one_swap.wait()
    other_in.wait()

    @pl.loop(0, width // TILE)
    def _(n):
        middle[:, tile_of(n)] += contract(got[...], lefts[0, tile_of(n), :], 1, 1)

    for index in range(2):
        part = slice(index * some, (index + 1) * some)
        of = pl.ds(pl.multiple_of(shard * own_tokens + index * some, some), some)
        if index:
            keep_in(index).start()
        keep_in(index).wait()
        factor = fac[of, 0:1]
        unit = tall[of, :].astype(F32) * factor
        scaled = middle[part, :] * gain_one
        inner = jnp.mean(scaled * unit, axis=-1, keepdims=True)
        cots[part, :] = (gin[0:some, :] + factor * (scaled - unit * inner)).astype(BF16)

    input_copy = pltpu.make_async_copy(cots, grad_input, out_sem.at[4])
    input_copy.start()
    layer_copies.append(layer_rows(1))
    run("z1")
    for copy in [input_copy] + layer_copies + result_copies(JOBS + 1):
        copy.wait()


def attention_back(
    later, gin, middle, cot, hiddens, w_ffn, w_late, w_other, forward, cos2, sin2, vector, tail
):
    w_attn, qrot, krot, vlow, lse, mixed, in_one_t, hid_all = forward
    own_tokens, width = cot.shape
    tokens = 2 * own_tokens
    heads = lse.shape[0]
    width_q = heads * HD
    width_qkv = width_q + 2 * HD
    side_rows, wide = later.shape[1:]
    rows = side_rows // CHIPS
    vmem = pl.BlockSpec(memory_space=pltpu.VMEM)
    hbm = pl.BlockSpec(memory_space=pl.ANY)
    dma = pltpu.SemaphoreType.DMA
    shape = jax.ShapeDtypeStruct
    half = (own_tokens, width)
    n_swaps = own_tokens // TILE + 3
    return pl.pallas_call(
        functools.partial(backward_kernel, (rows, heads, later.shape[0] - JOBS, tail)),
        in_specs=[hbm] * 16 + [vmem] * 3,
        out_specs=[hbm, hbm, vmem] + [hbm] * 6,
        out_shape=[
            shape(half, BF16), shape(half, BF16), shape((8, width), F32),
        ] + [shape((rows, (JOBS - 1) * CHUNK + tail), F32)] * 3 + [
            shape((rows, width_qkv), F32), shape((rows, width_q), F32), shape(half, F32),
        ],
        scratch_shapes=[
            pltpu.VMEM((3, side_rows, wide), BF16),
            pltpu.VMEM((3, HALF, 2, rows, wide), BF16),
            pltpu.VMEM((side_rows, width_qkv), BF16),
            pltpu.VMEM((side_rows, width_qkv), BF16),
            pltpu.VMEM((2, width, tokens), BF16),
            pltpu.VMEM(half, F32),
            pltpu.VMEM(half, F32),
            pltpu.VMEM((tokens, width), BF16),
            pltpu.VMEM(w_attn.shape, BF16),
            pltpu.VMEM((tokens, width_q), BF16),
            pltpu.VMEM((tokens, HD), BF16),
            pltpu.VMEM((tokens, HD), BF16),
            pltpu.VMEM(lse.shape, F32),
            pltpu.VMEM((tokens, width_q), BF16),
            pltpu.VMEM((tokens, width_q), BF16),
            pltpu.VMEM((tokens, width_qkv), BF16),
            pltpu.VMEM((tokens, HD), F32),
            pltpu.VMEM((tokens, HD), F32),
            pltpu.VMEM(half, BF16),
            pltpu.VMEM(half, BF16),
            pltpu.VMEM(half, BF16),
            pltpu.VMEM((own_tokens, width_qkv), BF16),
            pltpu.VMEM((rows, wide), F32),
            pltpu.VMEM((4, 8, width), F32),
            pltpu.VMEM((3, 4, 8, width), F32),
            dma((16,)), dma((3, HALF, 2, 3)), dma((3, HALF, 2, 3)), dma((2, 2)), dma((2, 2)),
            dma((n_swaps,)), dma((n_swaps,)), dma((7,)), dma((3, 3)), dma((3, 4)), dma((2,)), dma((2,)),
        ],
        compiler_params=pltpu.CompilerParams(
            collective_id=3, has_side_effects=True, vmem_limit_bytes=63 * 2**20
        ),
        cost_estimate=pl.CostEstimate(
            flops=10 * heads * tokens * tokens * HD, bytes_accessed=50 * 2**20, transcendentals=0
        ),
        name="attention_back",
    )(
        later, gin, middle, cot, hiddens, w_ffn, w_late, w_other, w_attn, qrot, krot, vlow, lse, mixed, in_one_t,
        hid_all, cos2, sin2, vector,
    )


def finish_kernel(
    layer_in, input_in, first_g, first_u, first_d, last_g, last_u, last_d, qkv_in, out_in, small_in,
    layer_out, grad_input, grad_q, grad_k, grad_v, grad_out, grad_g, grad_u, grad_d, vec_one, vec_two,
    bias_q, bias_k, bias_v,
    layer, grad, gates, ups, downs, qkv, out, in_sem, out_sem,
):
    early = first_g.shape[1]
    moves = [
        (layer_in, layer, layer_out), (input_in, grad, grad_input),
        (first_g, gates.at[:, 0:early], None), (last_g, gates.at[:, early:], None),
        (first_u, ups.at[:, 0:early], None), (last_u, ups.at[:, early:], None),
        (first_d, downs.at[:, 0:early], None), (last_d, downs.at[:, early:], None),
        (qkv_in, qkv, None), (out_in, out, grad_out),
    ]
    loads = [
        pltpu.make_async_copy(source, buffer, in_sem.at[i]) for i, (source, buffer, _) in enumerate(moves)
    ]
    for copy in loads:
        copy.start()
    stores = []

    def store(buffer, target):
        copy = pltpu.make_async_copy(buffer, target, out_sem.at[len(stores)])
        copy.start()
        stores.append(copy)

    for i, (_, buffer, target) in enumerate(moves):
        loads[i].wait()
        if target is not None:
            store(buffer, target)
        if i in (3, 5, 7):
            store(*((gates, grad_g), (ups, grad_u), (downs, grad_d))[i // 2 - 1])
    begin = 0
    for target in (grad_q, grad_k, grad_v):
        store(qkv.at[:, begin : begin + target.shape[1]], target)
        begin += target.shape[1]
    for i, target in enumerate((vec_one, vec_two, bias_q)):
        target[...] = small_in[i : i + 1, :].reshape(target.shape[0])
    wide = bias_k.shape[0]
    bias_k[...] = small_in[3:4, 0:wide].reshape(wide)
    bias_v[...] = small_in[3:4, wide : 2 * wide].reshape(wide)
    for copy in stores:
        copy.wait()


def finish(layer_out, grad_input, first, last, sum_qkv, sum_out, small, width_q):
    vmem = pl.BlockSpec(memory_space=pltpu.VMEM)
    hbm = pl.BlockSpec(memory_space=pl.ANY)
    shape = jax.ShapeDtypeStruct
    rows, width_qkv = sum_qkv.shape
    width_k = (width_qkv - width_q) // 2
    width = layer_out.shape[1]
    ffn = (rows, first[0].shape[1] + last[0].shape[1])
    dma = pltpu.SemaphoreType.DMA
    return pl.pallas_call(
        finish_kernel,
        in_specs=[hbm] * 10 + [vmem],
        out_specs=[hbm] * 9 + [vmem] * 5,
        out_shape=[
            shape(layer_out.shape, BF16), shape(grad_input.shape, BF16),
            shape((rows, width_q), F32), shape((rows, width_k), F32), shape((rows, width_k), F32),
            shape(sum_out.shape, F32), shape(ffn, F32), shape(ffn, F32), shape(ffn, F32),
            shape((width,), F32), shape((width,), F32), shape((2 * width_q,), F32),
            shape((2 * width_k,), F32), shape((2 * width_k,), F32),
        ],
        scratch_shapes=[
            pltpu.VMEM(layer_out.shape, BF16), pltpu.VMEM(grad_input.shape, BF16),
            pltpu.VMEM(ffn, F32), pltpu.VMEM(ffn, F32), pltpu.VMEM(ffn, F32),
            pltpu.VMEM(sum_qkv.shape, F32), pltpu.VMEM(sum_out.shape, F32), dma((10,)), dma((9,)),
        ],
        compiler_params=pltpu.CompilerParams(vmem_limit_bytes=62 * 2**20),
        name="finish",
    )(layer_out, grad_input, *first, *last, sum_qkv, sum_out, small)


def body_fused(
    hidden_in, positions, query_weight, query_bias, key_weight, key_bias, value_weight, value_bias,
    out_weight, gate_weight, up_weight, down_weight, attn_gain, ffn_gain, cotangent,
):
    rows, width_q = query_weight.shape
    heads = width_q // HD
    hidden_units = gate_weight.shape[1]
    own_tokens, width = hidden_in.shape
    half = HD // 2
    lanes = jnp.arange(HD, dtype=jnp.int32)
    freq = jnp.power(ROPE_BASE, -2.0 * (lanes % half).astype(F32) / HD)
    ffn_weights = (gate_weight, up_weight, down_weight.T)
    (w_ffn, w_attn, hidden_all, grad_ffn, in_one_t, qrot, krot, vlow, mixed, lse, middle,
     inputs_two, vector, cos2, sin2, in_two_t, cot_t) = forward_attention(
        hidden_in, cotangent,
        (freq, positions, query_bias, key_bias, value_bias, attn_gain, ffn_gain),
        (query_weight, key_weight, value_weight, out_weight.T, *ffn_weights),
        heads,
    )
    hiddens, grad_normed_two, later, *first_sums, w_other, w_late = feed_forward(
        inputs_two, grad_ffn, in_two_t, cot_t, w_ffn, w_attn, width_q + 2 * HD, ffn_weights
    )
    tail = units_of(-(-hidden_units // CHUNK) - 1, hidden_units)
    layer_out, grad_input, small, *sums = attention_back(
        later, grad_normed_two, middle, cotangent, hiddens, w_ffn, w_late, w_other,
        (w_attn, qrot, krot, vlow, lse, mixed, in_one_t, hidden_all), cos2, sin2, vector, tail,
    )
    (layer_out, grad_input, sum_q, sum_k, sum_v, sum_out, sum_gate, sum_up, sum_down, gain_one,
     gain_two, sum_bias_q, sum_bias_k, sum_bias_v) = finish(
        layer_out, grad_input, first_sums, sums[:3], *sums[3:5], small, width_q
    )
    return (
        layer_out,
        grad_input,
        sum_q,
        sum_bias_q,
        sum_k,
        sum_bias_k,
        sum_v,
        sum_bias_v,
        sum_out.T,
        sum_gate,
        sum_up,
        sum_down.T,
        gain_one,
        gain_two,
    )


def body(*arrays):
    rows = arrays[2].shape[0]
    if lax.axis_size("dp") == 2 * CHIPS and rows % 32 == 0 and -(-arrays[9].shape[1] // CHUNK) == 9:
        return body_fused(*arrays)
    return body_general(*arrays)


def solution(mesh):
    tokens, weight, weight_t = P(("dp", "mp"), None), P("dp", "mp"), P("mp", "dp")
    return jax.shard_map(
        body,
        mesh=mesh,
        in_specs=(
            tokens, P("dp"), weight, P(), weight, P(), weight, P(), weight_t,
            weight, weight, weight_t, P(), P(), tokens,
        ),
        out_specs=(
            tokens, tokens, weight, P(), weight, P(), weight, P(), weight_t,
            weight, weight, weight_t, P(), P(),
        ),
        check_vma=False,
    )
```

time: 2190 us -> 516 us (0.24)
  waiting for transfers between devices: 1650 us -> 0 us
  Pallas kernels: 0 us -> 508 us
  matrix products: 321 us -> 0 us
  blocking collectives: 83 us -> 0 us
  other arithmetic: 63.1 us -> 0.52 us
  local copies, waits for them, and re-layouts: 35.2 us -> 0 us
    reduce_scatter x11 -> x0, waiting for transfers between devices: 1190 us -> none  [the longest x1 267 us: body(): lax.psum_scatter(contract(inputs_two, grad_up, 0, 0), 'dp', scatter_dimen...]
    pallas_call x0 -> x4, Pallas kernels: none -> 508 us  [the longest x1 185 us: feed_forward(): pl.pallas_call(functools.partial(ffn_kernel, (rows, chunks, weights[0].sh...]
    all_gather x9 -> x0, waiting for transfers between devices: 457 us -> none  [the longest x1 111 us: body(): lax.all_gather(down_weight, 'dp', axis=1, tiled=True)]
    dot_general x35 -> x0, matrix products: 321 us -> none  [the longest x21 256 us: contract(): lax.dot_general(left, right, (((left_dim,), (right_dim,)), ((), ())), pre...]
    all_gather x2 -> x0, blocking collectives: 42.7 us -> none  [the longest x1 24.2 us: body(): lax.all_gather(key_weight, 'dp', axis=0, tiled=True)]
    psum x1 -> x0, blocking collectives: 40.3 us -> none  [body(): lax.psum((gain_one, gain_two, bias_query_part, bias_key_part, bias_value_...]
    reduce_sum x11 -> x0, other arithmetic: 24.1 us -> none  [the longest x2 7.53 us: attend_block(): total = jnp.sum(weights, axis=-1, keepdims=True)]
    convert_element_type x8 -> x0, other arithmetic: 23 us -> none  [the longest x2 10.1 us: attend_back(): grad_scores = (probs * (grad_probs - row_term)).astype(jnp.bfloat16)]
  transfers between devices with their start and end apart: 20 -> 0, of which waited for: 16 -> 0; matrix products, arithmetic and copies ran while one was open for 10% -> 0% of each run, Pallas kernels for 0% -> 0%
where the time goes in v1:
time: 516 us; the launch traced here: 509 us
  Pallas kernels  508 us (98%)
    pallas_call x1, Pallas kernels, feed_forward(): pl.pallas_call(functools.partial(ffn_kernel, (rows, chunks, weights[0].sh...  185 us
    pallas_call x1, Pallas kernels, forward_attention(): pl.pallas_call(functools.partial(forward_kernel, (rows, heads, units)), i...  176 us
    pallas_call x1, Pallas kernels, attention_back(): pl.pallas_call(functools.partial(backward_kernel, (rows, heads, later.sha...  139 us

profile of v1, /device:TPU:0, one launch (start us, length us, event | category | flops | bytes accessed | tf_op | source)
XLA Modules:
  0.0 509.4 jit_solution(7849137575154721014)
XLA Ops:
  0.6 0.5 fusion.2.turns
  1.2 176.1 %forward_attention.1 = (bf16[6,1536,1536]{2,1,0:T(8,128)(2,1)}, bf16[1536,1792]{1,0:T(8,128)(2,1)}, bf16[1024,1536]{1,0:T(8,128)(2,1)}, bf16[1024,1536]{1,0:T(8,...) custom-call(bf16[512,1536]{1,0:T(8,128)(2,1)} %hid.1, ...), custom_call_target="tpu_custom_call" | custom-call | flops 16911433728 | bytes 125829120 | tf_op jit(solution)/shard_map/forward_attention/pallas_call | solution.py:910
  177.3 184.8 %feed_forward.1 = (bf16[9,1024,512]{2,1,0:T(8,128)(2,1)}, f32[512,1536]{1,0:T(8,128)}, bf16[6,768,1536]{2,1,0:T(8,128)(2,1)}, f32[96,2560]{1,0:T(8,128)}, f32[96...) custom-call(bf16[1024,1536]{1,0:T(8,128)(2,1)} %get-tuple-element.61.in2_hbm, ...), custom_call_target="tpu_custom_call" | custom-call | flops 130459631616 | bytes 83886080 | tf_op jit(solution)/shard_map/feed_forward/pallas_call | solution.py:1413
  362.1 138.7 %attention_back.1 = (bf16[512,1536]{1,0:T(8,128)(2,1)}, bf16[512,1536]{1,0:T(8,128)(2,1)}, f32[8,1536]{1,0:T(8,128)}, f32[96,1920]{1,0:T(8,128)}, f32[96,1920]{1...) custom-call(bf16[6,768,1536]{2,1,0:T(8,128)(2,1)} %get-tuple-element.67.later, ...), custom_call_target="tpu_custom_call" | custom-call | flops 8053063680 | bytes 52428800 | tf_op jit(solution)/shard_map/attention_back/pallas_call | solution.py:1922
  500.8 8.2 %finish.1 = (bf16[512,1536]{1,0:T(8,128)(2,1)}, bf16[512,1536]{1,0:T(8,128)(2,1)}, f32[96,768]{1,0:T(8,128)}, f32[96,128]{1,0:T(8,128)}, f32[96,128]{1,0:T(8,128...) custom-call(bf16[512,1536]{1,0:T(8,128)(2,1)} %get-tuple-element.83., ...), custom_call_target="tpu_custom_call" | custom-call | tf_op jit(solution)/shard_map/finish/pallas_call | solution.py:2027

commit v2 on v1

--- a/solution.py
+++ b/solution.py
@@ -1055,10 +1055,10 @@
 
 def ffn_kernel(
     cfg, in2_hbm, cot_hbm, in2t_hbm, cott_hbm, w_ffn, w_attn, wg, wu, wd,
-    hiddens, gin_own, later, grad_g, grad_u, grad_d, w_other, w_late,
+    hiddens, w_down, gin_own, later, grad_g, grad_u, grad_d, w_other, w_late,
     in2, cot, in2t, cott, wbuf, acts, gin, own, sent, sib, ring, stage, pack,
     in_sem, w_sem, sib_send, sib_recv, ring_send, ring_recv, out_sem, g_sem, end_sem, free_sem,
-    pack_sem, store_sem, hop_send, hop_recv, side_send, side_recv, park_sem, fetch_sem, hid_sem,
+    pack_sem, store_sem, hop_send, hop_recv, side_send, side_recv, park_sem, fetch_sem, hid_sem, down_sem,
 ):
     rows, chunks, total = cfg
     grads = (grad_g, grad_u, grad_d)
@@ -1074,21 +1074,34 @@
     own_rows = pl.ds(pl.multiple_of(shard * own_tokens, TILE), own_tokens)
     other_rows = pl.ds(pl.multiple_of((1 - shard) * own_tokens, TILE), own_tokens)
 
-    def load(chunk, m):
-        columns = (slice(0, 2 * CHUNK), slice(2 * CHUNK, 3 * CHUNK))[m]
-        return pltpu.make_async_copy(
-            w_ffn.at[chunk, :, columns], wbuf.at[:, columns], w_sem.at[m]
-        )
-
     def size_of(i):
         return units_of(first + i, total)
 
-    def load_late(i, m):
-        size = size_of(i)
-        columns = (slice(0, 2 * size), slice(2 * size, 3 * size))[m]
-        return pltpu.make_async_copy(
-            w_late.at[i, :, columns], wbuf.at[:, columns], w_sem.at[m]
-        )
+    def load(chunk, s):
+        return pltpu.make_async_copy(w_ffn.at[chunk], wbuf.at[s], w_sem.at[s])
+
+    def load_late(i, s):
+        columns = slice(0, 3 * size_of(i))
+        return pltpu.make_async_copy(w_late.at[i, :, columns], wbuf.at[s, :, columns], w_sem.at[s])
+
+    def down_copies(chunk, s, size=CHUNK):
+        top = width // 2
+        return [
+            pltpu.make_async_copy(
+                wbuf.at[s, h * top : (h + 1) * top, 2 * size : 3 * size],
+                w_down.at[chunk, :, h * CHUNK : h * CHUNK + size], down_sem.at[s, h],
+            )
+            for h in range(2)
+        ]
+
+    def hidden_copies(index, chunk, size=CHUNK):
+        return [
+            pltpu.make_async_copy(
+                acts.at[index, h * own_tokens : (h + 1) * own_tokens, 2 * size : 3 * size],
+                hiddens.at[chunk, :, h * CHUNK : h * CHUNK + size], hid_sem.at[index, h],
+            )
+            for h in range(2)
+        ]
 
     def home(unit, member, half):
         return w_late.at[unit, here.part(member, half), 0 : 3 * size_of(unit)]
@@ -1133,7 +1146,7 @@
                     source.at[here.part(member), :], target.at[begin : begin + rows, :],
                     in_sem.at[2 + i],
                 ))
-    for copy in own_blocks + [load(0, m) for m in range(2)] + inputs:
+    for copy in own_blocks + [load(0, 0)] + inputs:
         copy.start()
     here.greet()
     for copy in own_blocks:
@@ -1213,29 +1226,24 @@
             device_id={"mp": 1 - shard}, device_id_type=MESH,
         )
 
-    def hidden_copy(index, chunk, size=CHUNK):
-        return pltpu.make_async_copy(
-            acts.at[index, :, 2 * size : 3 * size], hiddens.at[chunk, :, 0:size], hid_sem.at[index]
-        )
-
-    def forward(index, part, size=CHUNK):
+    def forward(index, part, s, size=CHUNK):
         for begin in range(0, size, TILE):
             stop = min(begin + TILE, size)
             gates, ups, downs = (slice(m * size + begin, m * size + stop) for m in range(3))
-            gate = contract(in2[part, :], wbuf[:, gates], 1, 0)
-            up = contract(in2[part, :], wbuf[:, ups], 1, 0)
-            grad = contract(cot[part, :], wbuf[:, downs], 1, 0)
+            gate = contract(in2[part, :], wbuf[s, :, gates], 1, 0)
+            up = contract(in2[part, :], wbuf[s, :, ups], 1, 0)
+            grad = contract(cot[part, :], wbuf[s, :, downs], 1, 0)
             sig = 0.5 * jnp.tanh(0.5 * gate) + 0.5
             swish = gate * sig
             acts[index, part, downs] = (swish * up).astype(BF16)
             acts[index, part, gates] = (grad * up * (sig + swish - swish * sig)).astype(BF16)
             acts[index, part, ups] = (grad * swish).astype(BF16)
 
-    def back_gin(index, part, size=CHUNK):
+    def back_gin(index, part, s, size=CHUNK):
         @pl.loop(0, width // TILE)
         def _(n):
             gin[part, tile_of(n)] += contract(
-                acts[index, part, 0 : 2 * size], wbuf[tile_of(n), 0 : 2 * size], 1, 1
+                acts[index, part, 0 : 2 * size], wbuf[s, tile_of(n), 0 : 2 * size], 1, 1
             )
 
     def weight_grads(index, p, between, size=CHUNK):
@@ -1269,54 +1277,50 @@
 
     weight_copy().start()
 
+    def start(copies):
+        for copy in copies:
+            copy.start()
+
+    def wait(copies):
+        for copy in copies:
+            copy.wait()
+
     @pl.loop(0, first)
     def _(j):
         p = lax.rem(j, 2)
-        for m in range(2):
-            load(j, m).wait()
+        load(j, p).wait()
+        start(down_copies(j, p))
 
         @pl.when(j >= 1)
         def _():
-            hidden_copy(0, j - 1).wait()
-
-        forward(0, slice(0, own_tokens))
-
-        @pl.when((j >= 1) & (j <= SETS))
+            wait(down_copies(j - 1, 1 - p))
+            wait(hidden_copies(0, j - 1))
+
+        @pl.when(j + 1 < first)
         def _():
-            park(j - 1, 1 - p, True).wait()
-
-        @pl.when(j > SETS)
-        def _():
-            park(j - 1, 1 - p, False).wait()
-
-        at_point(j, "a")
-        forward(0, slice(own_tokens, tokens))
-        hidden_copy(0, j).start()
-        at_point(j, "b")
+            load(j + 1, 1 - p).start()
 
         @pl.when(j == first - 1)
         def _():
             gather.end(0)
             gather.sent(0)
-
-        @pl.when(j + 1 < first)
+            load_late(0, 1 - p).start()
+
+        forward(0, slice(0, own_tokens), p)
+
+        @pl.when((j >= 1) & (j <= SETS))
         def _():
-            load(j + 1, 1).start()
-
-        @pl.when(j == first - 1)
+            park(j - 1, 1 - p, True).wait()
+
+        @pl.when(j > SETS)
         def _():
-            load_late(0, 1).start()
-
-        back_gin(0, slice(0, tokens))
-
-        @pl.when(j + 1 < first)
-        def _():
-            load(j + 1, 0).start()
-
-        @pl.when(j == first - 1)
-        def _():
-            load_late(0, 0).start()
-
+            park(j - 1, 1 - p, False).wait()
+
+        at_point(j, "a")
+        forward(0, slice(own_tokens, tokens), p)
+        start(hidden_copies(0, j))
+        at_point(j, "b")
+        back_gin(0, slice(0, tokens), p)
         at_point(j, "c")
 
         @pl.when(j == 0)
@@ -1336,7 +1340,8 @@
 
         at_point(j, "f")
 
-    hidden_copy(0, first - 1).wait()
+    wait(hidden_copies(0, first - 1))
+    wait(down_copies(first - 1, (first - 1) % 2))
     for unit in range(1, LATER):
         gather.end(unit)
         gather.sent(unit)
@@ -1345,22 +1350,20 @@
         part = (other_rows, own_rows)[half]
         for i in range(LATER):
             size = size_of(i)
-            for m in range(2):
-                load_late(i, m).wait()
-            forward(i, part, size)
+            turn = half * LATER + i
+            s = (first + turn) % 2
+            load_late(i, s).wait()
+            if half == 0:
+                start(down_copies(first + i, s, size))
+            if 0 < turn <= LATER:
+                wait(down_copies(first + turn - 1, 1 - s, size_of(turn - 1)))
+            if turn + 1 < 2 * LATER:
+                load_late((i + 1) % LATER, 1 - s).start()
+            forward(i, part, s, size)
             if half == 1:
-                hidden_copy(i, first + i, size).start()
+                start(hidden_copies(i, first + i, size))
             run(EVENTS.get((first + half, f"{i}a"), ""))
-            following = i + 1 if i + 1 < LATER else 0
-            same = size_of(following) == size
-            more = half == 0 or i + 1 < LATER
-            if more and same:
-                load_late(following, 1).start()
-            back_gin(i, part, size)
-            if more:
-                load_late(following, 0).start()
-            if more and not same:
-                load_late(following, 1).start()
+            back_gin(i, part, s, size)
             run(EVENTS.get((first + half, f"{i}b"), ""))
         if half == 0:
             pl.semaphore_signal(
@@ -1397,7 +1400,7 @@
     for copy in [gin_out, last_park] + result_copies(rings - 1):
         copy.wait()
     for i in range(LATER):
-        hidden_copy(i, first + i, size_of(i)).wait()
+        wait(hidden_copies(i, first + i, size_of(i)))
 
 
 def feed_forward(inputs_two, grad_ffn, in_two_t, cot_t, w_ffn, w_attn, width_qkv, weights):
@@ -1413,9 +1416,10 @@
     return pl.pallas_call(
         functools.partial(ffn_kernel, (rows, chunks, weights[0].shape[1])),
         in_specs=[hbm] * 9,
-        out_specs=[hbm] * 8,
+        out_specs=[hbm] * 9,
         out_shape=[
-            shape((chunks, tokens, CHUNK), BF16), shape(half, F32),
+            shape((chunks, tokens // 2, 2 * CHUNK), BF16),
+            shape((chunks, width // 2, 2 * CHUNK), BF16), shape(half, F32),
             shape((chunks - SETS, side_rows, wide), BF16),
         ] + [shape((rows, (chunks - LATER - 1) * CHUNK), F32)] * 3 + [
             shape((width, width_qkv), BF16),
@@ -1426,7 +1430,7 @@
             pltpu.VMEM((tokens, width), BF16),
             pltpu.VMEM((width, tokens), BF16),
             pltpu.VMEM((width, tokens), BF16),
-            pltpu.VMEM((width, wide), BF16),
+            pltpu.VMEM((2, width, wide), BF16),
             pltpu.VMEM((LATER, tokens, wide), BF16),
             pltpu.VMEM((tokens, width), F32),
             pltpu.VMEM((SETS, side_rows, wide), BF16),
@@ -1439,7 +1443,7 @@
             dma((2, HALF, 2, 3)), dma((2, HALF, 2, 3)), dma((3,)), dma((4,)), dma((1,)),
             pltpu.SemaphoreType.REGULAR,
             dma((LATER, 3)), dma((LATER, pieces)), dma((LATER, HALF, 2)), dma((LATER, HALF, 2)),
-            dma((LATER, pieces)), dma((LATER, pieces)), dma((2,)), dma((SETS,)), dma((LATER,)),
+            dma((LATER, pieces)), dma((LATER, pieces)), dma((2,)), dma((SETS,)), dma((LATER, 2)), dma((2, 2)),
         ],
         compiler_params=pltpu.CompilerParams(
             collective_id=2, has_side_effects=True, vmem_limit_bytes=63 * 2**20
@@ -1482,7 +1486,7 @@
 
 
 def backward_kernel(
-    cfg, later, gin_hbm, middle_hbm, cot_hbm, hiddens, w_ffn, w_late, w_other, w_attn, qrot_hbm, krot_hbm,
+    cfg, later, gin_hbm, middle_hbm, cot_hbm, hiddens, w_down, w_other, w_attn, qrot_hbm, krot_hbm,
     vlow_hbm, lse_hbm, mixed_hbm, in_one_t, hid_hbm, cos_ref, sin_ref, vec_ref,
     layer_out, grad_input, small_out, grad_g, grad_u, grad_d, grad_qkv, grad_out, kept,
     own, ring, sent, sib, lefts, gin, middle, tall, wa, qrot, krot, vlow, lse, mixed,
@@ -1638,21 +1642,23 @@
     keep.start()
     keep.wait()
     middle[...] = jnp.zeros_like(middle)
-    early = w_ffn.shape[0]
-    chunks = early + w_late.shape[0]
+    chunks = w_down.shape[0]
+    top = width // 2
 
     def down_in(chunk):
-        size = CHUNK if chunk + 1 < chunks else tail
-        slot = chunk % 2 * CHUNK
-        source = w_ffn.at[chunk] if chunk < early else w_late.at[chunk - early]
+        slot = chunk % 2
+        weight_to = lefts.at[1, slot * top : (slot + 1) * top, :]
+        hidden_to = dqkv.at[slot * own_tokens : (slot + 1) * own_tokens, :]
+        if chunk + 1 < chunks:
+            parts = [slice(0, 2 * CHUNK)]
+        else:
+            parts = [slice(h * CHUNK, h * CHUNK + tail) for h in range(2)]
         return [
-            pltpu.make_async_copy(
-                source.at[:, 2 * size : 3 * size], lefts.at[1, :, slot : slot + size],
-                down_sem.at[chunk % 2],
-            ),
-            pltpu.make_async_copy(
-                hiddens.at[chunk, :, 0:size], dqkv.at[:, slot : slot + size], hid_sem.at[chunk % 2]
-            ),
+            pltpu.make_async_copy(source.at[chunk, :, part], target.at[:, part], sem.at[slot, i])
+            for i, part in enumerate(parts)
+            for source, target, sem in (
+                (w_down, weight_to, down_sem), (hiddens, hidden_to, hid_sem)
+            )
         ]
 
     for copy in down_in(0):
@@ -1663,14 +1669,19 @@
                 copy.start()
         for copy in down_in(chunk):
             copy.wait()
-        begin = chunk % 2 * CHUNK
-        columns = slice(begin, begin + (CHUNK if chunk + 1 < chunks else tail))
-
-        @pl.loop(0, width // TILE)
-        def _(n):
-            weight = lefts[1, tile_of(n), columns]
-            middle[:, tile_of(n)] += contract(dqkv[other_rows, columns], weight, 1, 1)
-            gin[:, tile_of(n)] += contract(dqkv[own_rows, columns], weight, 1, 1)
+        slot, size = chunk % 2, CHUNK if chunk + 1 < chunks else tail
+        part = slice(slot * own_tokens, (slot + 1) * own_tokens)
+        own_columns, other_columns = (
+            pl.ds(pl.multiple_of(side * CHUNK, CHUNK), size) for side in (shard, 1 - shard)
+        )
+        for h in range(2):
+            @pl.loop(0, top // TILE)
+            def _(n):
+                rows_of = pl.ds(pl.multiple_of(slot * top + n * TILE, TILE), TILE)
+                at = pl.ds(pl.multiple_of(h * top + n * TILE, TILE), TILE)
+                weight = lefts[1, rows_of, h * CHUNK : h * CHUNK + size]
+                middle[:, at] += contract(dqkv[part, other_columns], weight, 1, 1)
+                gin[:, at] += contract(dqkv[part, own_columns], weight, 1, 1)
 
         run(f"w{chunk}")
 
@@ -1903,7 +1914,7 @@
 
 
 def attention_back(
-    later, gin, middle, cot, hiddens, w_ffn, w_late, w_other, forward, cos2, sin2, vector, tail
+    later, gin, middle, cot, hiddens, w_down, w_other, forward, cos2, sin2, vector, tail
 ):
     w_attn, qrot, krot, vlow, lse, mixed, in_one_t, hid_all = forward
     own_tokens, width = cot.shape
@@ -1921,7 +1932,7 @@
     n_swaps = own_tokens // TILE + 3
     return pl.pallas_call(
         functools.partial(backward_kernel, (rows, heads, later.shape[0] - JOBS, tail)),
-        in_specs=[hbm] * 16 + [vmem] * 3,
+        in_specs=[hbm] * 15 + [vmem] * 3,
         out_specs=[hbm, hbm, vmem] + [hbm] * 6,
         out_shape=[
             shape(half, BF16), shape(half, BF16), shape((8, width), F32),
@@ -1955,7 +1966,7 @@
             pltpu.VMEM((4, 8, width), F32),
             pltpu.VMEM((3, 4, 8, width), F32),
             dma((16,)), dma((3, HALF, 2, 3)), dma((3, HALF, 2, 3)), dma((2, 2)), dma((2, 2)),
-            dma((n_swaps,)), dma((n_swaps,)), dma((7,)), dma((3, 3)), dma((3, 4)), dma((2,)), dma((2,)),
+            dma((n_swaps,)), dma((n_swaps,)), dma((7,)), dma((3, 3)), dma((3, 4)), dma((2, 2)), dma((2, 2)),
         ],
         compiler_params=pltpu.CompilerParams(
             collective_id=3, has_side_effects=True, vmem_limit_bytes=63 * 2**20
@@ -1965,7 +1976,7 @@
         ),
         name="attention_back",
     )(
-        later, gin, middle, cot, hiddens, w_ffn, w_late, w_other, w_attn, qrot, krot, vlow, lse, mixed, in_one_t,
+        later, gin, middle, cot, hiddens, w_down, w_other, w_attn, qrot, krot, vlow, lse, mixed, in_one_t,
         hid_all, cos2, sin2, vector,
     )
 
@@ -2064,12 +2075,12 @@
         (query_weight, key_weight, value_weight, out_weight.T, *ffn_weights),
         heads,
     )
-    hiddens, grad_normed_two, later, *first_sums, w_other, w_late = feed_forward(
+    hiddens, w_down, grad_normed_two, later, *first_sums, w_other, _ = feed_forward(
         inputs_two, grad_ffn, in_two_t, cot_t, w_ffn, w_attn, width_q + 2 * HD, ffn_weights
     )
     tail = units_of(-(-hidden_units // CHUNK) - 1, hidden_units)
     layer_out, grad_input, small, *sums = attention_back(
-        later, grad_normed_two, middle, cotangent, hiddens, w_ffn, w_late, w_other,
+        later, grad_normed_two, middle, cotangent, hiddens, w_down, w_other,
         (w_attn, qrot, krot, vlow, lse, mixed, in_one_t, hidden_all), cos2, sin2, vector, tail,
     )
     (layer_out, grad_input, sum_q, sum_k, sum_v, sum_out, sum_gate, sum_up, sum_down, gain_one,

time: 516 us -> 513 us (level)
  no operation moved by 1% of the time
where the time goes in v2:
time: 513 us; the launch traced here: 506 us
  Pallas kernels  505 us (98%)
    pallas_call x1, Pallas kernels, feed_forward(): pl.pallas_call(functools.partial(ffn_kernel, (rows, chunks, weights[0].sh...  183 us
    pallas_call x1, Pallas kernels, forward_attention(): pl.pallas_call(functools.partial(forward_kernel, (rows, heads, units)), i...  176 us
    pallas_call x1, Pallas kernels, attention_back(): pl.pallas_call(functools.partial(backward_kernel, (rows, heads, later.sha...  138 us

profile of v2, /device:TPU:0, one launch (start us, length us, event | category | flops | bytes accessed | tf_op | source)
XLA Modules:
  0.0 506.2 jit_solution(5448376872901120012)
XLA Ops:
  0.6 0.5 fusion.2.turns
  1.2 176.1 %forward_attention.1 = (bf16[6,1536,1536]{2,1,0:T(8,128)(2,1)}, bf16[1536,1792]{1,0:T(8,128)(2,1)}, bf16[1024,1536]{1,0:T(8,128)(2,1)}, bf16[1024,1536]{1,0:T(8,...) custom-call(bf16[512,1536]{1,0:T(8,128)(2,1)} %hid.1, ...), custom_call_target="tpu_custom_call" | custom-call | flops 16911433728 | bytes 125829120 | tf_op jit(solution)/shard_map/forward_attention/pallas_call | solution.py:910
  177.3 182.6 %feed_forward.1 = (bf16[9,512,1024]{2,1,0:T(8,128)(2,1)}, bf16[9,768,1024]{2,1,0:T(8,128)(2,1)}, f32[512,1536]{1,0:T(8,128)}, bf16[6,768,1536]{2,1,0:T(8,128)(2,...) custom-call(bf16[1024,1536]{1,0:T(8,128)(2,1)} %get-tuple-element.61, ...), custom_call_target="tpu_custom_call" | custom-call | flops 130459631616 | bytes 83886080 | tf_op jit(solution)/shard_map/feed_forward/pallas_call | solution.py:1416
  359.9 137.6 %attention_back.1 = (bf16[512,1536]{1,0:T(8,128)(2,1)}, bf16[512,1536]{1,0:T(8,128)(2,1)}, f32[8,1536]{1,0:T(8,128)}, f32[96,1920]{1,0:T(8,128)}, f32[96,1920]{1...) custom-call(bf16[6,768,1536]{2,1,0:T(8,128)(2,1)} %get-tuple-element.67.later, ...), custom_call_target="tpu_custom_call" | custom-call | flops 8053063680 | bytes 52428800 | tf_op jit(solution)/shard_map/attention_back/pallas_call | solution.py:1933
  497.5 8.2 %finish.1 = (bf16[512,1536]{1,0:T(8,128)(2,1)}, bf16[512,1536]{1,0:T(8,128)(2,1)}, f32[96,768]{1,0:T(8,128)}, f32[96,128]{1,0:T(8,128)}, f32[96,128]{1,0:T(8,128...) custom-call(bf16[512,1536]{1,0:T(8,128)(2,1)} %get-tuple-element.83., ...), custom_call_target="tpu_custom_call" | custom-call | tf_op jit(solution)/shard_map/finish/pallas_call | solution.py:2038

commit v3 on v2

--- a/solution.py
+++ b/solution.py
@@ -1505,7 +1505,7 @@
     shard, me = here.shard, here.me
     sums = Sums(here, own, ring, ring_send, ring_recv)
     wide_qkv, wide_out = (2, width_qkv // 2), (2, width_q // 2)
-    pieces = [(3, CHUNK)] * (JOBS - 1) + [(3, tail), wide_qkv, wide_out]
+    pieces = [(1, 3 * CHUNK)] * (JOBS - 1) + [(1, 3 * tail), (1, width_qkv), (1, width_q)]
     own_rows = pl.ds(pl.multiple_of(shard * own_tokens, TILE), own_tokens)
     other_rows = pl.ds(pl.multiple_of((1 - shard) * own_tokens, TILE), own_tokens)
 
@@ -1579,13 +1579,13 @@
 
     def result_copies(job):
         if job < JOBS:
-            count, size = pieces[job]
+            size = CHUNK if job + 1 < JOBS else tail
             return [
                 pltpu.make_async_copy(
                     stage.at[:, m * size : (m + 1) * size],
                     grads[m].at[:, job * CHUNK : job * CHUNK + size], out_sem.at[m],
                 )
-                for m in range(count)
+                for m in range(3)
             ]
         target = (grad_qkv, grad_out)[job - JOBS]
         return [pltpu.make_async_copy(stage.at[:, 0 : target.shape[1]], target, out_sem.at[0])]

time: 513 us -> 512 us (level)
  no operation moved by 1% of the time
where the time goes in v3:
time: 512 us; the launch traced here: 506 us
  Pallas kernels  504 us (98%)
    pallas_call x1, Pallas kernels, feed_forward(): pl.pallas_call(functools.partial(ffn_kernel, (rows, chunks, weights[0].sh...  183 us
    pallas_call x1, Pallas kernels, forward_attention(): pl.pallas_call(functools.partial(forward_kernel, (rows, heads, units)), i...  176 us
    pallas_call x1, Pallas kernels, attention_back(): pl.pallas_call(functools.partial(backward_kernel, (rows, heads, later.sha...  137 us

profile of v3, /device:TPU:0, one launch (start us, length us, event | category | flops | bytes accessed | tf_op | source)
XLA Modules:
  0.0 505.9 jit_solution(7244424718007323937)
XLA Ops:
  0.6 0.5 fusion.2.turns
  1.2 176.1 %forward_attention.1 = (bf16[6,1536,1536]{2,1,0:T(8,128)(2,1)}, bf16[1536,1792]{1,0:T(8,128)(2,1)}, bf16[1024,1536]{1,0:T(8,128)(2,1)}, bf16[1024,1536]{1,0:T(8,...) custom-call(bf16[512,1536]{1,0:T(8,128)(2,1)} %hid.1, ...), custom_call_target="tpu_custom_call" | custom-call | flops 16911433728 | bytes 125829120 | tf_op jit(solution)/shard_map/forward_attention/pallas_call | solution.py:910
  177.3 182.6 %feed_forward.1 = (bf16[9,512,1024]{2,1,0:T(8,128)(2,1)}, bf16[9,768,1024]{2,1,0:T(8,128)(2,1)}, f32[512,1536]{1,0:T(8,128)}, bf16[6,768,1536]{2,1,0:T(8,128)(2,...) custom-call(bf16[1024,1536]{1,0:T(8,128)(2,1)} %get-tuple-element.61, ...), custom_call_target="tpu_custom_call" | custom-call | flops 130459631616 | bytes 83886080 | tf_op jit(solution)/shard_map/feed_forward/pallas_call | solution.py:1416
  359.9 137.3 %attention_back.1 = (bf16[512,1536]{1,0:T(8,128)(2,1)}, bf16[512,1536]{1,0:T(8,128)(2,1)}, f32[8,1536]{1,0:T(8,128)}, f32[96,1920]{1,0:T(8,128)}, f32[96,1920]{1...) custom-call(bf16[6,768,1536]{2,1,0:T(8,128)(2,1)} %get-tuple-element.67.later, ...), custom_call_target="tpu_custom_call" | custom-call | flops 8053063680 | bytes 52428800 | tf_op jit(solution)/shard_map/attention_back/pallas_call | solution.py:1933
  497.3 8.2 %finish.1 = (bf16[512,1536]{1,0:T(8,128)(2,1)}, bf16[512,1536]{1,0:T(8,128)(2,1)}, f32[96,768]{1,0:T(8,128)}, f32[96,128]{1,0:T(8,128)}, f32[96,128]{1,0:T(8,128...) custom-call(bf16[512,1536]{1,0:T(8,128)(2,1)} %get-tuple-element.83., ...), custom_call_target="tpu_custom_call" | custom-call | tf_op jit(solution)/shard_map/finish/pallas_call | solution.py:2038

commit v4 on v3

--- a/solution.py
+++ b/solution.py
@@ -1095,13 +1095,9 @@
         ]
 
     def hidden_copies(index, chunk, size=CHUNK):
-        return [
-            pltpu.make_async_copy(
-                acts.at[index, h * own_tokens : (h + 1) * own_tokens, 2 * size : 3 * size],
-                hiddens.at[chunk, :, h * CHUNK : h * CHUNK + size], hid_sem.at[index, h],
-            )
-            for h in range(2)
-        ]
+        return [pltpu.make_async_copy(
+            acts.at[index, :, 2 * size : 3 * size], hiddens.at[chunk, :, 0:size], hid_sem.at[index]
+        )]
 
     def home(unit, member, half):
         return w_late.at[unit, here.part(member, half), 0 : 3 * size_of(unit)]
@@ -1418,7 +1414,7 @@
         in_specs=[hbm] * 9,
         out_specs=[hbm] * 9,
         out_shape=[
-            shape((chunks, tokens // 2, 2 * CHUNK), BF16),
+            shape((chunks, tokens, CHUNK), BF16),
             shape((chunks, width // 2, 2 * CHUNK), BF16), shape(half, F32),
             shape((chunks - SETS, side_rows, wide), BF16),
         ] + [shape((rows, (chunks - LATER - 1) * CHUNK), F32)] * 3 + [
@@ -1443,7 +1439,7 @@
             dma((2, HALF, 2, 3)), dma((2, HALF, 2, 3)), dma((3,)), dma((4,)), dma((1,)),
             pltpu.SemaphoreType.REGULAR,
             dma((LATER, 3)), dma((LATER, pieces)), dma((LATER, HALF, 2)), dma((LATER, HALF, 2)),
-            dma((LATER, pieces)), dma((LATER, pieces)), dma((2,)), dma((SETS,)), dma((LATER, 2)), dma((2, 2)),
+            dma((LATER, pieces)), dma((LATER, pieces)), dma((2,)), dma((SETS,)), dma((LATER,)), dma((2, 2)),
         ],
         compiler_params=pltpu.CompilerParams(
             collective_id=2, has_side_effects=True, vmem_limit_bytes=63 * 2**20
@@ -1633,13 +1629,13 @@
         inner = jnp.mean(scaled * unit, axis=-1, keepdims=True)
         total = cots[part, :].astype(F32) + factor * (scaled - unit * inner)
         middle[part, :] = total
-        gin[part, :] = v
         tall[at_own(t), :] = total.astype(BF16)
         attn_swap(t).start()
         small[0, 1:2, :] += jnp.sum(e * unit, axis=0, keepdims=True)
 
     keep = pltpu.make_async_copy(middle, kept, out_sem.at[5])
     keep.start()
+    gin[...] = jnp.zeros_like(gin)
     keep.wait()
     middle[...] = jnp.zeros_like(middle)
     chunks = w_down.shape[0]
@@ -1648,18 +1644,21 @@
     def down_in(chunk):
         slot = chunk % 2
         weight_to = lefts.at[1, slot * top : (slot + 1) * top, :]
-        hidden_to = dqkv.at[slot * own_tokens : (slot + 1) * own_tokens, :]
+        size = CHUNK if chunk + 1 < chunks else tail
         if chunk + 1 < chunks:
             parts = [slice(0, 2 * CHUNK)]
         else:
             parts = [slice(h * CHUNK, h * CHUNK + tail) for h in range(2)]
-        return [
-            pltpu.make_async_copy(source.at[chunk, :, part], target.at[:, part], sem.at[slot, i])
+        copies = [
+            pltpu.make_async_copy(
+                w_down.at[chunk, :, part], weight_to.at[:, part], down_sem.at[slot, i]
+            )
             for i, part in enumerate(parts)
-            for source, target, sem in (
-                (w_down, weight_to, down_sem), (hiddens, hidden_to, hid_sem)
-            )
         ]
+        return copies + [pltpu.make_async_copy(
+            hiddens.at[chunk, :, 0:size], dqkv.at[:, slot * CHUNK : slot * CHUNK + size],
+            hid_sem.at[slot],
+        )]
 
     for copy in down_in(0):
         copy.start()
@@ -1670,24 +1669,34 @@
         for copy in down_in(chunk):
             copy.wait()
         slot, size = chunk % 2, CHUNK if chunk + 1 < chunks else tail
-        part = slice(slot * own_tokens, (slot + 1) * own_tokens)
-        own_columns, other_columns = (
-            pl.ds(pl.multiple_of(side * CHUNK, CHUNK), size) for side in (shard, 1 - shard)
-        )
+        part = slice(slot * CHUNK, slot * CHUNK + size)
         for h in range(2):
             @pl.loop(0, top // TILE)
             def _(n):
                 rows_of = pl.ds(pl.multiple_of(slot * top + n * TILE, TILE), TILE)
                 at = pl.ds(pl.multiple_of(h * top + n * TILE, TILE), TILE)
                 weight = lefts[1, rows_of, h * CHUNK : h * CHUNK + size]
-                middle[:, at] += contract(dqkv[part, other_columns], weight, 1, 1)
-                gin[:, at] += contract(dqkv[part, own_columns], weight, 1, 1)
+                product = contract(dqkv[:, part], weight, 1, 1)
+                middle[:, at] += product[0:own_tokens, :]
+                gin[:, at] += product[own_tokens:, :]
 
         run(f"w{chunk}")
 
-    osend[...] = middle[...].astype(BF16)
+    @pl.loop(0, half_tiles)
+    def _(t):
+        one, two = middle[tile_of(t), :], gin[tile_of(t), :]
+        osend[tile_of(t), :] = jnp.where(shard == 0, two, one).astype(BF16)
+        gin[tile_of(t), :] = jnp.where(shard == 0, one, two)
+
     out_swap(0).start()
+    middle_in = get(4, middle_hbm, middle)
+    middle_in.start()
     run("w9")
+    middle_in.wait()
+
+    @pl.loop(0, half_tiles)
+    def _(t):
+        gin[tile_of(t), :] += middle[tile_of(t), :]
 
     for copy in rest_in:
         copy.wait()
@@ -1966,7 +1975,7 @@
             pltpu.VMEM((4, 8, width), F32),
             pltpu.VMEM((3, 4, 8, width), F32),
             dma((16,)), dma((3, HALF, 2, 3)), dma((3, HALF, 2, 3)), dma((2, 2)), dma((2, 2)),
-            dma((n_swaps,)), dma((n_swaps,)), dma((7,)), dma((3, 3)), dma((3, 4)), dma((2, 2)), dma((2, 2)),
+            dma((n_swaps,)), dma((n_swaps,)), dma((7,)), dma((3, 3)), dma((3, 4)), dma((2, 2)), dma((2,)),
         ],
         compiler_params=pltpu.CompilerParams(
             collective_id=3, has_side_effects=True, vmem_limit_bytes=63 * 2**20

time: 512 us -> 512 us (level)
  no operation moved by 1% of the time
where the time goes in v4:
time: 512 us; the launch traced here: 506 us
  Pallas kernels  504 us (98%)
    pallas_call x1, Pallas kernels, feed_forward(): pl.pallas_call(functools.partial(ffn_kernel, (rows, chunks, weights[0].sh...  183 us
    pallas_call x1, Pallas kernels, forward_attention(): pl.pallas_call(functools.partial(forward_kernel, (rows, heads, units)), i...  176 us
    pallas_call x1, Pallas kernels, attention_back(): pl.pallas_call(functools.partial(backward_kernel, (rows, heads, later.sha...  137 us

profile of v4, /device:TPU:0, one launch (start us, length us, event | category | flops | bytes accessed | tf_op | source)
XLA Modules:
  0.0 505.7 jit_solution(10577287331961975592)
XLA Ops:
  0.6 0.5 fusion.2.turns
  1.2 176.1 %forward_attention.1 = (bf16[6,1536,1536]{2,1,0:T(8,128)(2,1)}, bf16[1536,1792]{1,0:T(8,128)(2,1)}, bf16[1024,1536]{1,0:T(8,128)(2,1)}, bf16[1024,1536]{1,0:T(8,...) custom-call(bf16[512,1536]{1,0:T(8,128)(2,1)} %hid.1, ...), custom_call_target="tpu_custom_call" | custom-call | flops 16911433728 | bytes 125829120 | tf_op jit(solution)/shard_map/forward_attention/pallas_call | solution.py:910
  177.3 182.6 %feed_forward.1 = (bf16[9,1024,512]{2,1,0:T(8,128)(2,1)}, bf16[9,768,1024]{2,1,0:T(8,128)(2,1)}, f32[512,1536]{1,0:T(8,128)}, bf16[6,768,1536]{2,1,0:T(8,128)(2,...) custom-call(bf16[1024,1536]{1,0:T(8,128)(2,1)} %get-tuple-element.61, ...), custom_call_target="tpu_custom_call" | custom-call | flops 130459631616 | bytes 83886080 | tf_op jit(solution)/shard_map/feed_forward/pallas_call | solution.py:1412
  359.9 137.1 %attention_back.1 = (bf16[512,1536]{1,0:T(8,128)(2,1)}, bf16[512,1536]{1,0:T(8,128)(2,1)}, f32[8,1536]{1,0:T(8,128)}, f32[96,1920]{1,0:T(8,128)}, f32[96,1920]{1...) custom-call(bf16[6,768,1536]{2,1,0:T(8,128)(2,1)} %get-tuple-element.67.later, ...), custom_call_target="tpu_custom_call" | custom-call | flops 8053063680 | bytes 52428800 | tf_op jit(solution)/shard_map/attention_back/pallas_call | solution.py:1942
  497.1 8.2 %finish.1 = (bf16[512,1536]{1,0:T(8,128)(2,1)}, bf16[512,1536]{1,0:T(8,128)(2,1)}, f32[96,768]{1,0:T(8,128)}, f32[96,128]{1,0:T(8,128)}, f32[96,128]{1,0:T(8,128...) custom-call(bf16[512,1536]{1,0:T(8,128)(2,1)} %get-tuple-element.83., ...), custom_call_target="tpu_custom_call" | custom-call | tf_op jit(solution)/shard_map/finish/pallas_call | solution.py:2047

commit v5 on v4

--- a/solution.py
+++ b/solution.py
@@ -1472,11 +1472,14 @@
     "t1": "24",
     "t2": "32",
     "t3": "41",
-    "g": "33",
-    "b": "42",
-    "u1": "50 34 43",
-    "l0": "51",
-    "l2": "44 52 53",
+    "u0": "33",
+    "u1": "50",
+    "f": "42",
+    "g": "34 51",
+    "b": "43",
+    "l0": "52",
+    "l1": "44",
+    "l2": "53",
     "z1": "54",
 }
 
@@ -1799,6 +1802,10 @@
         attn_swap(t).wait_send()
     hid_in = get(15, hid_hbm, tall)
     hid_in.start()
+    send_side(1, 1, mixed, wide_out)
+    run("u0")
+    own_side(1, 1, mixed, wide_out, 2)
+    run("u1")
 
     fac = gk
     hid_in.wait()
@@ -1864,12 +1871,6 @@
         small[group + 1] = total
 
     small_start(0)
-    send_side(1, 1, mixed, wide_out)
-    run("u0")
-    own_side(1, 1, mixed, wide_out, 2)
-    small_end(0)
-    small_start(1)
-    run("u1")
 
     def layer_rows(index):
         part = slice(index * some, (index + 1) * some)
@@ -1887,6 +1888,8 @@
 
     layer_copies = [layer_rows(0)]
     keep_in(0).start()
+    small_end(0)
+    small_start(1)
     run("l0")
     small_end(1)
     small_start(2)

time: 512 us -> 505 us (0.986)
  Pallas kernels: 504 us -> 497 us
    pallas_call x1, Pallas kernels: 137 us -> 130 us  [attention_back(): pl.pallas_call(functools.partial(backward_kernel, (rows, heads, later.sha...]
where the time goes in v5:
time: 505 us; the launch traced here: 498 us
  Pallas kernels  497 us (98%)
    pallas_call x1, Pallas kernels, feed_forward(): pl.pallas_call(functools.partial(ffn_kernel, (rows, chunks, weights[0].sh...  183 us
    pallas_call x1, Pallas kernels, forward_attention(): pl.pallas_call(functools.partial(forward_kernel, (rows, heads, units)), i...  176 us
    pallas_call x1, Pallas kernels, attention_back(): pl.pallas_call(functools.partial(backward_kernel, (rows, heads, later.sha...  130 us

profile of v5, /device:TPU:0, one launch (start us, length us, event | category | flops | bytes accessed | tf_op | source)
XLA Modules:
  0.0 498.5 jit_solution(9841587908893925361)
XLA Ops:
  0.6 0.5 fusion.2.turns
  1.2 176.1 %forward_attention.1 = (bf16[6,1536,1536]{2,1,0:T(8,128)(2,1)}, bf16[1536,1792]{1,0:T(8,128)(2,1)}, bf16[1024,1536]{1,0:T(8,128)(2,1)}, bf16[1024,1536]{1,0:T(8,...) custom-call(bf16[512,1536]{1,0:T(8,128)(2,1)} %hid.1, ...), custom_call_target="tpu_custom_call" | custom-call | flops 16911433728 | bytes 125829120 | tf_op jit(solution)/shard_map/forward_attention/pallas_call | solution.py:910
  177.3 182.6 %feed_forward.1 = (bf16[9,1024,512]{2,1,0:T(8,128)(2,1)}, bf16[9,768,1024]{2,1,0:T(8,128)(2,1)}, f32[512,1536]{1,0:T(8,128)}, bf16[6,768,1536]{2,1,0:T(8,128)(2,...) custom-call(bf16[1024,1536]{1,0:T(8,128)(2,1)} %get-tuple-element.61, ...), custom_call_target="tpu_custom_call" | custom-call | flops 130459631616 | bytes 83886080 | tf_op jit(solution)/shard_map/feed_forward/pallas_call | solution.py:1412
  359.9 129.9 %attention_back.1 = (bf16[512,1536]{1,0:T(8,128)(2,1)}, bf16[512,1536]{1,0:T(8,128)(2,1)}, f32[8,1536]{1,0:T(8,128)}, f32[96,1920]{1,0:T(8,128)}, f32[96,1920]{1...) custom-call(bf16[6,768,1536]{2,1,0:T(8,128)(2,1)} %get-tuple-element.67.later, ...), custom_call_target="tpu_custom_call" | custom-call | flops 8053063680 | bytes 52428800 | tf_op jit(solution)/shard_map/attention_back/pallas_call | solution.py:1945
  489.8 8.2 %finish.1 = (bf16[512,1536]{1,0:T(8,128)(2,1)}, bf16[512,1536]{1,0:T(8,128)(2,1)}, f32[96,768]{1,0:T(8,128)}, f32[96,128]{1,0:T(8,128)}, f32[96,128]{1,0:T(8,128...) custom-call(bf16[512,1536]{1,0:T(8,128)(2,1)} %get-tuple-element.83., ...), custom_call_target="tpu_custom_call" | custom-call | tf_op jit(solution)/shard_map/finish/pallas_call | solution.py:2050
